TPU v7x, 128 devices: a whole 4x4x4 slice. The times are simulated.
128 devices in a mesh: col: 16 (over x, y), row: 8 (over z, core).
Axes of the slice: x: 4, y: 4, z: 4, core: 2. Of those that a mesh axis runs over, the one named last changes fastest.
Arguments:
- raw_counts: bfloat16 [512, 4096, 256], P('row', 'col'), may hold values from -35 to 60
- gain_class: int32 [512, 4096], P('row', 'col'), may hold values from 0 to 15
- good_pixels: int32 [512, 4096], P('row', 'col'), may hold values 0 or 1
- class_gains: float32 [16, 256], replicated, may hold values from 0.6 to 1.6
Outputs:
- whitened: bfloat16 [512, 4096, 256], P('row', 'col')
- noise_field: bfloat16 [512, 4096, 256], P('row', 'col')
- factor: float32 [256, 256], replicated
All inputs are finite; a program needn't handle non-finite values. No bound on the sum of `good_pixels` on one device may be relied on, other than what follows from the above.
Results may differ from a plain program's by a relative error of at most 0.002.
Values sent between devices are 32-bit elements; how exact they have to be, the bound alone decides.
No kernel may reach another device: no remote copies, remote signals or barrier semaphores. Data moves between devices by JAX's collectives and lax.ppermute only.
A program may use at most 256 MiB of HBM per device.

v0:
```python
import jax
import jax.numpy as jnp
from jax import lax
from jax.sharding import PartitionSpec as P


def shifted(value, axis, steps):
    count = lax.axis_size(axis)
    leading, last = (max(0, -steps), min(count, count - steps))
    return lax.ppermute(value, axis, [(source, source + steps) for source in range(leading, last)])


def products(left, right):
    return lax.dot_general(left, right, (((0,), (0,)), ((), ())), precision=lax.Precision.HIGHEST)


def on_device(raw_counts, gain_class, good_pixels, class_gains):
    rows_here, cols_here, channels = raw_counts.shape
    classes = class_gains.shape[0]
    pixels = rows_here * cols_here
    onehot = (
        jnp.arange(classes, dtype=jnp.int32)[:, None] == gain_class.reshape(1, pixels)
    ).astype(jnp.float32)
    gain_map = products(onehot, class_gains).reshape(rows_here, cols_here, channels)
    valid = good_pixels.astype(jnp.float32)
    calibrated = raw_counts.astype(jnp.float32) * gain_map * valid[..., None]
    below_vals, below_valid = shifted((calibrated[:1], valid[:1]), "row", -1)
    right_vals, right_valid = shifted((calibrated[:, :1], valid[:, :1]), "col", -1)
    down_next = jnp.concatenate([calibrated[1:], below_vals], 0)
    down_w = valid * jnp.concatenate([valid[1:], below_valid], 0)
    right_next = jnp.concatenate([calibrated[:, 1:], right_vals], 1)
    right_w = valid * jnp.concatenate([valid[:, 1:], right_valid], 1)
    down_diff = (down_next - calibrated) * down_w[..., None]
    right_diff = (right_next - calibrated) * right_w[..., None]
    flat_down = down_diff.reshape(pixels, channels)
    flat_right = right_diff.reshape(pixels, channels)
    noise_local = products(flat_down, flat_down) + products(flat_right, flat_right)
    pixel_sum = jnp.sum(calibrated.reshape(pixels, channels), axis=0)
    noise_sum, total_sum, count, pairs = lax.psum(
        (noise_local, pixel_sum, jnp.sum(valid), jnp.sum(down_w) + jnp.sum(right_w)), ("col", "row")
    )
    noise_cov = noise_sum / (2.0 * pairs)
    mean = total_sum / count
    lower = jnp.linalg.cholesky(noise_cov)
    identity = jnp.eye(channels, dtype=lower.dtype)
    inverse = lax.linalg.triangular_solve(lower, identity, left_side=True, lower=True)
    centred = (calibrated - mean) * valid[..., None]
    whitened = jnp.dot(
        centred.reshape(pixels, channels), inverse.T, precision=lax.Precision.HIGHEST
    ).astype(jnp.bfloat16)
    noise_flat = jnp.dot(flat_down + flat_right, inverse.T, precision=lax.Precision.HIGHEST).astype(
        jnp.bfloat16
    )
    gram_local = lax.dot_general(
        whitened, whitened, (((0,), (0,)), ((), ())), preferred_element_type=jnp.float32
    )
    gram_sum = lax.psum(gram_local, ("col", "row"))
    factor = jnp.linalg.cholesky(gram_sum / count).T
    return (
        whitened.reshape(rows_here, cols_here, channels),
        noise_flat.reshape(rows_here, cols_here, channels),
        factor,
    )


def solution(mesh):
    return jax.shard_map(
        on_device,
        mesh=mesh,
        in_specs=(P("row", "col", None), P("row", "col"), P("row", "col"), P()),
        out_specs=(P("row", "col", None), P("row", "col", None), P()),
        check_vma=False,
    )
```

profile of v0, /device:TPU:1, one launch (start us, length us, event | category | flops | bytes accessed | tf_op | source)
XLA Modules:
  0.0 609.3 jit_solution(804126603412660734)
XLA Ops:
  9.4 3.3 collective-permute-start.1
  13.6 6.8 %fusion.16 = f32[16384,256]{1,0:T(8,128)S(1)} fusion(f32[16,256]{1,0:T(8,128)S(1)} %copy-done, s32[16384]{0:T(1024)S(1)} %bitcast.69), kind=kOutput, calls=%fused_computation.20 | convolution fusion | flops 805568512 | bytes 16859136 | tf_op jit(solution)/shard_map/dot_general | solution.py:14
  20.4 5.4 fusion.36
  27.2 1.9 collective-permute-start
  29.3 7.3 %slice.81 = f32[64,255,256]{2,1,0:T(8,128)} slice(f32[64,256,256]{2,1,0:T(8,128)S(1)} %get-tuple-element.31), slice={[0:64], [1:256], [0:256]} | slice | bytes 33423360 | tf_op jit(solution)/shard_map/slice | solution.py:31
  36.5 6.4 %slice.77 = f32[63,256,256]{2,1,0:T(8,128)} slice(f32[64,256,256]{2,1,0:T(8,128)S(1)} %get-tuple-element.31), slice={[1:64], [0:256], [0:256]} | slice | bytes 33030144 | tf_op jit(solution)/shard_map/slice | solution.py:29
  44.9 71.0 %all-reduce.1 = (f32[256]{0:T(256)S(1)}, f32[]{:T(128)}, f32[]{:T(128)}) all-reduce(f32[256]{0:T(256)S(1)} %get-tuple-element.30, f32[]{:T(128)} %get-tuple-element.44, f32[]{:T(128)S(6)} %add.41), channel_id=1, replica_groups=mesh['col'=16,'row'=8] {'col','row'}, use_global_device_ids=true, to_apply=%region_1.0 | all-reduce | flops 258 | bytes 2064 | tf_op jit(solution)/shard_map/psum | solution.py:39
  117.3 39.1 %fusion.7 = f32[256,256]{0,1:T(8,128)S(1)} fusion(f32[64,256,256]{2,1,0:T(8,128)} %copy-done.2, f32[64,1,256]{2,1,0:T(1,128)S(1)} %collective-permute-done.2, f32[64,255,256]{2,1,0:T(8,128)} %slice.81, f32[64,256]{1,0:T(8,128)S(1)} %get-tuple-element.27), kind=kOutput, calls=%fused_computation.13 | convolution fusion | flops 12897484800 | bytes 33882112 | tf_op jit(solution)/shard_map/dot_general | solution.py:14
  156.4 39.8 %fusion.13 = f32[256,256]{0,1:T(8,128)} fusion(f32[256,256]{0,1:T(8,128)S(1)} %fusion.7, f32[64,256,256]{2,1,0:T(8,128)S(1)} %copy-done.3, f32[1,256,256]{2,1,0:T(8,128)S(1)} %collective-permute-done, f32[63,256,256]{2,1,0:T(8,128)} %slice.77, f32[64,256]{1,0:T(8,128)S(1)} %get-tuple-element.46), kind=kOutput, calls=%fused_computation.15 | convolution fusion | flops 12897550336 | bytes 34144256 | tf_op jit(solution)/shard_map/dot_general | solution.py:14
  196.7 27.7 %fusion.2 = (f32[64,256,256]{2,1,0:T(8,128)}, f32[64,256,256]{2,1,0:T(8,128)}) fusion(f32[64,256]{1,0:T(8,128)S(1)} %get-tuple-element.46, f32[64,256,256]{2,1,0:T(8,128)} %copy-done.2, f32[1,256,256]{2,1,0:T(8,128)S(1)} %collective-permute-done, f32[63,256,256]{2,1,0:T(8,128)} %slice.77, f32[64,256]{1,0:T(8,128)S(1)} %get-tuple-element.27, ...), kind=kLoop, calls=%fused_computation.10 | loop fusion | flops 37748736 | bytes 84083712 | tf_op jit(solution)/shard_map/add | solution.py:51
  224.3 110.8 %all-reduce.5.cloned.1.call-done = f32[256,256]{0,1:T(8,128)} async-done(((f32[256,256]{0,1:T(8,128)}), f32[256,256]{0,1:T(8,128)}) %all-reduce.5.cloned.1.call-update) | async-done | bytes 262160 | tf_op jit(solution)/shard_map/psum | solution.py:39
  337.3 11.7 %cholesky.130 = f32[128,128]{1,0:T(8,128)S(1)} custom-call(f32[128,128]{1,0:T(8,128)S(1)} %cholesky.194), custom_call_target="Cholesky" | custom-call | tf_op jit(solution)/shard_map/jit(cholesky)/cholesky | solution.py:44
  349.1 9.8 %custom-call.13 = f32[1,128,128]{1,2,0:T(8,128)S(1)} custom-call(f32[1,128,128]{2,1,0:T(8,128)S(1)} %get-tuple-element.43), custom_call_target="InvertDiagBlocksLowerTriangular" | custom-call | tf_op jit(solution)/shard_map/jit(cholesky)/cholesky | solution.py:44
  359.4 11.7 %cholesky.147 = f32[128,128]{1,0:T(8,128)S(1)} custom-call(f32[128,128]{1,0:T(8,128)S(1)} %convolution_subtract_fusion.2), custom_call_target="Cholesky" | custom-call | tf_op jit(solution)/shard_map/jit(cholesky)/cholesky | solution.py:44
  373.2 4.0 while.1
  377.1 19.8 %custom-call.11 = f32[2,128,128]{1,2,0:T(8,128)S(1)} custom-call(f32[2,128,128]{2,1,0:T(8,128)S(1)} %get-tuple-element.11), custom_call_target="InvertDiagBlocksLowerTriangular" | custom-call | tf_op jit(solution)/shard_map/triangular_solve | solution.py:46
  397.9 16.9 %convolution_convert_fusion.1 = bf16[16384,256]{1,0:T(8,128)(2,1)S(1)} fusion(f32[16384,256]{1,0:T(8,128)} %bitcast.66, f32[128,256]{1,0:T(8,128)S(1)} %fusion.25, f32[128,256]{1,0:T(8,128)S(1)} %fusion.20), kind=kOutput, calls=%fused_computation.3 | convolution fusion | flops 12889161728 | bytes 25427968 | tf_op jit(solution)/shard_map/dot_general | solution.py:48
  414.8 3.4 copy-done.4
  418.1 4.1 fusion.38
  422.2 17.5 %convolution_convert_fusion = bf16[16384,256]{1,0:T(8,128)(2,1)} fusion(f32[16384,256]{1,0:T(8,128)} %bitcast.65, f32[128,256]{1,0:T(8,128)S(1)} %fusion.25, f32[128,256]{1,0:T(8,128)S(1)} %fusion.20), kind=kOutput, calls=%fused_computation.2 | convolution fusion | flops 12889161728 | bytes 25427968 | tf_op jit(solution)/shard_map/dot_general | solution.py:51
  439.7 121.7 %all-reduce.7.cloned.1.call-done = f32[256,256]{0,1:T(8,128)} async-done(((f32[256,256]{0,1:T(8,128)}), f32[256,256]{0,1:T(8,128)}) %all-reduce.7.cloned.1.call-update) | async-done | bytes 262160 | tf_op jit(solution)/shard_map/psum | solution.py:57
  564.8 11.7 %cholesky.164 = f32[128,128]{1,0:T(8,128)S(1)} custom-call(f32[128,128]{1,0:T(8,128)S(1)} %cholesky.197), custom_call_target="Cholesky" | custom-call | tf_op jit(solution)/shard_map/jit(cholesky)/cholesky | solution.py:58
  576.6 9.8 %custom-call.14 = f32[1,128,128]{1,2,0:T(8,128)S(1)} custom-call(f32[1,128,128]{2,1,0:T(8,128)S(1)} %get-tuple-element.39), custom_call_target="InvertDiagBlocksLowerTriangular" | custom-call | tf_op jit(solution)/shard_map/jit(cholesky)/cholesky | solution.py:58
  586.9 11.7 %cholesky.181 = f32[128,128]{1,0:T(8,128)S(1)} custom-call(f32[128,128]{1,0:T(8,128)S(1)} %convolution_subtract_fusion.1), custom_call_target="Cholesky" | custom-call | tf_op jit(solution)/shard_map/jit(cholesky)/cholesky | solution.py:58
  (68 shorter events, 20.8 us)
Async XLA Ops:
  7.2 6.4 %copy-start = (f32[16,256]{1,0:T(8,128)S(1)}, f32[16,256]{1,0:T(8,128)}, u32[]{:S(2)}) copy-start(f32[16,256]{1,0:T(8,128)} %param.8) | copy-start | bytes 49156
  7.2 328.0 %all-reduce.5.cloned.1.call-start = ((), (), s32[]{:S(2)}) async-start(), calls=%async_computation | async-start | bytes 524288 | tf_op jit(solution)/shard_map/psum | solution.py:39
  8.1 34.8 %collective-permute-start.3 = (f32[64,1]{1,0:T(8,128)S(1)}, f32[64,1]{1,0:T(8,128)S(1)}, u32[]{:S(2)}, u32[]{:S(2)}) collective-permute-start(f32[64,1]{1,0:T(8,128)S(1)} %slice.84), channel_id=1, source_target_pairs={{8,0},{16,8},{24,16},{32,24},{40,32},{48,40},{56,48},{64,56},{72,6... | collective-permute-start | bytes 776 | tf_op jit(solution)/shard_map/ppermute | solution.py:10
  9.4 33.5 %collective-permute-start.1 = (f32[1,256]{1,0:T(1,128)S(1)}, f32[1,256]{1,0:T(1,128)S(1)}, u32[]{:S(2)}, u32[]{:S(2)}) collective-permute-start(f32[1,256]{1,0:T(1,128)S(1)} %slice.80), channel_id=1, source_target_pairs={{1,0},{2,1},{3,2},{4,3},{5,4},{6,5},{7,6},{9,8},{10,9},{11,10},{12... | collective-permute-start | bytes 3080 | tf_op jit(solution)/shard_map/ppermute | solution.py:10
  25.8 10.7 %copy-start.2 = (f32[64,256,256]{2,1,0:T(8,128)}, f32[64,256,256]{2,1,0:T(8,128)S(1)}, u32[]{:S(2)}) copy-start(f32[64,256,256]{2,1,0:T(8,128)S(1)} %get-tuple-element.31) | copy-start | bytes 50331652
  25.9 91.4 %collective-permute-start.2 = (f32[64,1,256]{2,1,0:T(1,128)S(1)}, f32[64,1,256]{2,1,0:T(1,128)S(1)}, u32[]{:S(2)}, u32[]{:S(2)}) collective-permute-start(f32[64,1,256]{2,1,0:T(1,128)S(1)} %slice.82), channel_id=1, source_target_pairs={{8,0},{16,8},{24,16},{32,24},{40,32},{48,40},{56,48},{64,56},{72,6... | collective-permute-start | bytes 196616 | tf_op jit(solution)/shard_map/ppermute | solution.py:10
  27.2 129.2 %collective-permute-start = (f32[1,256,256]{2,1,0:T(8,128)S(1)}, f32[1,256,256]{2,1,0:T(8,128)S(1)}, u32[]{:S(2)}, u32[]{:S(2)}) collective-permute-start(f32[1,256,256]{2,1,0:T(8,128)S(1)} %slice.78), channel_id=1, source_target_pairs={{1,0},{2,1},{3,2},{4,3},{5,4},{6,5},{7,6},{9,8},{10,9},{11,10},{12... | collective-permute-start | bytes 786440 | tf_op jit(solution)/shard_map/ppermute | solution.py:10
  36.5 6.4 %copy-start.5 = (s32[64,256]{1,0:T(8,128)S(1)}, s32[64,256]{1,0:T(8,128)}, u32[]{:S(2)}) copy-start(s32[64,256]{1,0:T(8,128)} %param.7) | copy-start | bytes 196612
  117.3 39.1 %copy-start.3 = (f32[64,256,256]{2,1,0:T(8,128)S(1)}, f32[64,256,256]{2,1,0:T(8,128)}, u32[]{:S(2)}) copy-start(f32[64,256,256]{2,1,0:T(8,128)} %copy-done.2) | copy-start | bytes 50331652
  196.2 365.2 %all-reduce.7.cloned.1.call-start = ((), (), s32[]{:S(2)}) async-start(), calls=%async_computation.1 | async-start | bytes 524288 | tf_op jit(solution)/shard_map/psum | solution.py:57
  414.7 3.4 copy-start.4
  422.2 180.0 %copy-start.1 = (f32[16,256]{1,0:T(8,128)S(1)}, f32[16,256]{1,0:T(8,128)}, u32[]{:S(2)}) copy-start(f32[16,256]{1,0:T(8,128)} %param.8) | copy-start | bytes 49156
Sparse Core Ops, SparseCore 0:
  196.3 138.7 all-reduce.4
  422.3 138.9 all-reduce.6
where the time goes:
time: 617 us; the launch traced here: 609 us
  waiting for transfers between devices  233 us (38%)
  other arithmetic  129 us (21%)
  matrix products  126 us (20%)
  blocking collectives  71 us (12%)
  local copies, waits for them, and re-layouts  23.3 us (4%)
  between operations  19.2 us (3%)
  starting transfers between devices  8.32 us (1%)
    psum x1, waiting for transfers between devices, on_device(): gram_sum = lax.psum(gram_local, ('col', 'row'))  122 us
    psum x1, waiting for transfers between devices, on_device(): lax.psum((noise_local, pixel_sum, jnp.sum(valid), jnp.sum(down_w) + jnp.s...  111 us
    dot_general x3, matrix products, products(): lax.dot_general(left, right, (((0,), (0,)), ((), ())), precision=lax.Prec...  85.6 us
    psum x1, blocking collectives, on_device(): lax.psum((noise_local, pixel_sum, jnp.sum(valid), jnp.sum(down_w) + jnp.s...  71 us
    another operation x7, other arithmetic, on_device(): factor = jnp.linalg.cholesky(gram_sum / count).T  34.7 us
    another operation x6, other arithmetic, on_device(): lower = jnp.linalg.cholesky(noise_cov)  33.9 us
    add x1, other arithmetic, on_device(): flat_down + flat_right  27.7 us
    another operation x3, other arithmetic, on_device(): lax.linalg.triangular_solve(lower, identity, left_side=True, lower=True)  19.9 us
  transfers between devices with their start and end apart: 6, of which 2 were waited for; matrix products, arithmetic and copies ran while one was open for 18% of the time, Pallas kernels for 0%

commit v1 on v0

v1 whole, which is shorter than its diff:
```python
import jax
import jax.numpy as jnp
from jax import lax
from jax.experimental import pallas as pl
from jax.experimental.pallas import tpu as pltpu
from jax.sharding import PartitionSpec as P

STEP_ROWS = 8
CHUNK = 32
HALF = 128
HIGHEST = lax.Precision.HIGHEST
F32 = jnp.float32
BF16 = jnp.bfloat16


def over_pixels(left, right):
    return lax.dot_general(left, right, (((0,), (0,)), ((), ())), preferred_element_type=F32)


def exact(left, right, left_dim=1, right_dim=0):
    return lax.dot_general(
        left,
        right,
        (((left_dim,), (right_dim,)), ((), ())),
        precision=HIGHEST,
        preferred_element_type=F32,
    )


def split(value):
    high = value.astype(BF16)
    return high, (value - high.astype(F32)).astype(BF16)


def stacked_gains(gains):
    high = gains.astype(BF16)
    rest = gains - high.astype(F32)
    middle = rest.astype(BF16)
    low = (rest - middle.astype(F32)).astype(BF16)
    return jnp.concatenate([high, middle, low], 0)


def row_gains(classes, valid, gains, count):
    which = lax.rem(lax.broadcasted_iota(jnp.int32, (3 * count, classes.shape[1]), 0), count)
    onehot = jnp.where((which == classes) & (valid > 0), 1.0, 0.0).astype(BF16)
    return over_pixels(onehot, gains)


def as_column(row):
    return jnp.transpose(jnp.broadcast_to(row, (8, row.shape[1])))[:, :1]


def edges_kernel(row_ref, col_ref, class_ref, valid_ref, gains_ref, row_out, col_out):
    count = gains_ref.shape[0]
    gains = stacked_gains(gains_ref[...])
    cols = row_ref.shape[1]
    rows = col_ref.shape[0]
    calibrated = row_ref[0].astype(F32) * row_gains(class_ref[0:1, :], valid_ref[0:1, :], gains, count)
    row_out[0:cols, :] = calibrated
    row_out[cols:, :] = jnp.broadcast_to(valid_ref[0:1, :].astype(F32), (8, cols))
    which = lax.rem(lax.broadcasted_iota(jnp.int32, (rows, 3 * count), 1), count)
    first_valid = valid_ref[:, 0:1]
    onehot = jnp.where((which == class_ref[:, 0:1]) & (first_valid > 0), 1.0, 0.0).astype(BF16)
    gain_col = jnp.dot(onehot, gains, preferred_element_type=F32)
    channels = gain_col.shape[1]
    raw_col = col_ref[...].astype(F32)[:, 0, :]
    col_out[:, :channels] = raw_col * gain_col
    col_out[:, channels:] = jnp.broadcast_to(first_valid.astype(F32), (rows, 128))


def edges(raw_counts, gain_class, good_pixels, class_gains):
    rows, cols, channels = raw_counts.shape
    whole = lambda shape: pl.BlockSpec(shape, lambda i: (0,) * len(shape))
    return pl.pallas_call(
        edges_kernel,
        grid=(1,),
        in_specs=[
            whole((1, cols, channels)),
            whole((rows, 16, channels)),
            whole((rows, cols)),
            whole((rows, cols)),
            whole(class_gains.shape),
        ],
        out_specs=[whole((cols + 8, channels)), whole((rows, channels + 128))],
        out_shape=[
            jax.ShapeDtypeStruct((cols + 8, channels), F32),
            jax.ShapeDtypeStruct((rows, channels + 128), F32),
        ],
        name="edges",
    )(raw_counts, raw_counts, gain_class, good_pixels, class_gains)


def moments_kernel(
    raw_ref, class_ref, valid_ref, gains_ref, high_ref, low_ref, products_ref, sums_ref, pivot_ref, plain, half_degree, terms, gains_bf
):
    step = pl.program_id(0)
    count = gains_ref.shape[0]
    rows, cols = valid_ref.shape
    channels = raw_ref.shape[2]

    @pl.when(step == 0)
    def _():
        valid = valid_ref[...].astype(F32)
        zero_row = jnp.zeros((1, cols), F32)
        zero_col = jnp.zeros((rows, 1), F32)
        degree = jnp.concatenate([valid[1:], zero_row], 0) + jnp.concatenate([zero_row, valid[:-1]], 0)
        degree = degree + jnp.concatenate([valid[:, 1:], zero_col], 1) + jnp.concatenate([zero_col, valid[:, :-1]], 1)
        half_degree[...] = 0.5 * degree
        plain[...] = jnp.zeros_like(plain)
        products_ref[...] = jnp.zeros_like(products_ref)
        sums_ref[...] = jnp.zeros_like(sums_ref)
        gains_bf[...] = stacked_gains(gains_ref[...])
        gain_map = row_gains(class_ref[0:1, :], valid_ref[0:1, :], gains_bf[...], count)
        number = jnp.maximum(jnp.sum(valid[0:1, :], keepdims=True), 1.0)
        pivot = jnp.sum(raw_ref[0].astype(F32) * gain_map, 0, keepdims=True) / number
        pivot_ref[...] = jnp.broadcast_to(pivot, pivot_ref.shape)

    start = pl.multiple_of(step * STEP_ROWS, STEP_ROWS)
    classes = class_ref[pl.ds(start, STEP_ROWS), :]
    valid = valid_ref[pl.ds(start, STEP_ROWS), :]
    degrees = jnp.transpose(half_degree[pl.ds(start, STEP_ROWS), :])
    valid_cols = jnp.transpose(valid.astype(F32))
    pivot = pivot_ref[0:1, :]
    gains = gains_bf[...]
    total = sums_ref[...]
    for row in range(STEP_ROWS):
        gain_map = row_gains(classes[row : row + 1], valid[row : row + 1], gains, count)
        for at in range(0, cols, CHUNK):
            calibrated = raw_ref[row, at : at + CHUNK, :].astype(F32) * gain_map[at : at + CHUNK]
            calibrated = calibrated - valid_cols[at : at + CHUNK, row : row + 1] * pivot
            high, low = split(calibrated)
            high_ref[row, at : at + CHUNK, :] = high
            low_ref[row, at : at + CHUNK, :] = low
            plain[row % 2, 8 + at : 8 + at + CHUNK, :] = calibrated
            left = plain[row % 2, 7 + at : 7 + at + CHUNK, :]
            above = plain[1 - row % 2, 8 + at : 8 + at + CHUNK, :]
            term = above + left - degrees[at : at + CHUNK, row : row + 1] * calibrated
            terms[row * cols + at : row * cols + at + CHUNK, :] = term.astype(BF16)
            total = total + jnp.sum(calibrated.reshape(CHUNK // 8, 8, channels), 0)
    sums_ref[...] = total
    pixels = STEP_ROWS * cols
    high = high_ref[...].reshape(pixels, channels)
    products_ref[...] += over_pixels(high, jnp.concatenate([terms[...], high], 1))


def moments(raw_counts, gain_class, good_pixels, class_gains):
    rows, cols, channels = raw_counts.shape
    whole = lambda shape: pl.BlockSpec(shape, lambda i: (0,) * len(shape))
    block = pl.BlockSpec((STEP_ROWS, cols, channels), lambda i: (i, 0, 0))
    pixels = rows * cols
    return pl.pallas_call(
        moments_kernel,
        grid=(rows // STEP_ROWS,),
        in_specs=[block, whole((rows, cols)), whole((rows, cols)), whole(class_gains.shape)],
        out_specs=[block, block, whole((channels, 2 * channels)), whole((8, channels)), whole((8, channels))],
        out_shape=[
            pltpu.HBM(raw_counts.shape, BF16),
            pltpu.HBM(raw_counts.shape, BF16),
            jax.ShapeDtypeStruct((channels, 2 * channels), F32),
            jax.ShapeDtypeStruct((8, channels), F32),
            jax.ShapeDtypeStruct((8, channels), F32),
        ],
        scratch_shapes=[
            pltpu.VMEM((2, 8 + cols, channels), F32),
            pltpu.VMEM((rows, cols), F32),
            pltpu.VMEM((STEP_ROWS * cols, channels), BF16),
            pltpu.VMEM((3 * class_gains.shape[0], channels), BF16),
        ],
        compiler_params=pltpu.CompilerParams(vmem_limit_bytes=32 * 1024 * 1024),
        cost_estimate=pl.CostEstimate(
            flops=10 * pixels * channels * channels, bytes_accessed=6 * pixels * channels, transcendentals=0
        ),
        name="moments",
    )(raw_counts, gain_class, good_pixels, class_gains)


def pack_kernel(
    products_ref, sums_ref, pivot_ref, below_ref, right_ref, high_row, low_row, high_col, low_col, valid_ref, packed_ref
):
    rows, cols = valid_ref.shape
    channels = sums_ref.shape[1]
    valid = valid_ref[...].astype(F32)
    last_valid = as_column(valid[rows - 1 : rows, :])
    below_row = below_ref[cols : cols + 1, :]
    below_valid = as_column(below_row)
    mine = high_row[0].astype(F32) + low_row[0].astype(F32)
    pivot = pivot_ref[0:1, :]
    down = last_valid * (below_ref[0:cols, :] - below_valid * pivot) - below_valid * mine
    right_valid = right_ref[:, channels : channels + 1]
    mine = (high_col[...].astype(F32) + low_col[...].astype(F32))[:, 15, :]
    last_col = valid[:, cols - 1 : cols]
    right = last_col * (right_ref[:, :channels] - right_valid * pivot) - right_valid * mine
    edge = jnp.concatenate([down, right], 0).astype(BF16)
    cross = products_ref[:, :channels]
    noise = over_pixels(edge, edge) - (cross + jnp.transpose(cross))
    number = jnp.sum(valid, keepdims=True)
    total = jnp.sum(sums_ref[...], 0, keepdims=True)
    shift = total + number * pivot
    second = products_ref[:, channels:] + (as_column(pivot) * shift + as_column(total) * pivot)
    total = shift
    at = 0
    for matrix in (noise, second):
        for part in (matrix[:HALF, :HALF], matrix[:HALF, HALF:], matrix[HALF:, HALF:]):
            packed_ref[at : at + HALF, :] = part
            at += HALF
    pairs = jnp.sum(valid[1:] * valid[:-1], keepdims=True) + jnp.sum(valid[:, 1:] * valid[:, :-1], keepdims=True)
    pairs = pairs + jnp.sum(valid[rows - 1 :] * below_row, keepdims=True)
    pairs = pairs + jnp.sum(last_col * right_valid, keepdims=True)
    line = lax.broadcasted_iota(jnp.int32, (8, HALF), 0)
    packed_ref[at : at + 8, :] = jnp.where(
        line == 0,
        total[:, :HALF],
        jnp.where(line == 1, total[:, HALF:], jnp.where(line == 2, number, jnp.where(line == 3, pairs, 0.0))),
    )
    packed_ref[at + 8 :, :] = jnp.zeros((packed_ref.shape[0] - at - 8, HALF), F32)


def pack(products, sums, pivot, below, right, high, low, good_pixels, length):
    rows, cols, channels = high.shape
    whole = lambda shape: pl.BlockSpec(shape, lambda i: (0,) * len(shape))
    last_row = pl.BlockSpec((1, cols, channels), lambda i: (rows - 1, 0, 0))
    last_col = pl.BlockSpec((rows, 16, channels), lambda i: (0, cols // 16 - 1, 0))
    return pl.pallas_call(
        pack_kernel,
        grid=(1,),
        in_specs=[
            whole(products.shape),
            whole(sums.shape),
            whole(pivot.shape),
            whole(below.shape),
            whole(right.shape),
            last_row,
            last_row,
            last_col,
            last_col,
            whole((rows, cols)),
        ],
        out_specs=whole((length, HALF)),
        out_shape=jax.ShapeDtypeStruct((length, HALF), F32),
        compiler_params=pltpu.CompilerParams(vmem_limit_bytes=32 * 1024 * 1024),
        name="pack",
    )(products, sums, pivot, below, right, high, low, high, low, good_pixels)


def inverse_of_pair(a, b, c):
    scale = 1.0 / (a * c - b * b)
    return c * scale, -(b * scale), a * scale


def eliminate(jobs):
    lane = lax.broadcasted_iota(jnp.int32, (8, HALF), 1)
    line = lax.broadcasted_iota(jnp.int32, (8, HALF), 0)
    spread = lambda value: jnp.broadcast_to(value, (8, HALF))
    pick = lambda value, place: jnp.take_along_axis(
        value, jnp.full((8, HALF), place, jnp.int32), axis=1, mode="promise_in_bounds"
    )
    tiles = HALF // 8
    done = [([None] * tiles, [None] * tiles) for _ in jobs]
    for turn in range(HALF // 4):
        tile, first, at = turn // 2, 4 * (turn % 2), 4 * turn
        for job, (done_main, done_extra) in zip(jobs, done):
            main, extra = job["main"], job["extra"]
            lead = main[tile]
            rows = [spread(lead[first + i : first + i + 1, :]) for i in range(4)]
            p = {(i, j): pick(rows[i], at + j) for i in range(4) for j in range(i, 4)}
            if job["inverse"]:
                inside = (lane >= at) & (lane < at + 4)
                rows = [jnp.where(inside, jnp.where(lane == at + i, 1.0, 0.0), row) for i, row in enumerate(rows)]
            more = [spread(extra[tile][first + i : first + i + 1, :]) for i in range(4)] if extra else None
            e00, e01, e11 = inverse_of_pair(p[0, 0], p[0, 1], p[1, 1])
            f00 = e00 * p[0, 2] + e01 * p[1, 2]
            f10 = e01 * p[0, 2] + e11 * p[1, 2]
            f01 = e00 * p[0, 3] + e01 * p[1, 3]
            f11 = e01 * p[0, 3] + e11 * p[1, 3]
            g00, g01, g11 = inverse_of_pair(
                p[2, 2] - (p[0, 2] * f00 + p[1, 2] * f10),
                p[2, 3] - (p[0, 2] * f01 + p[1, 2] * f11),
                p[3, 3] - (p[0, 3] * f01 + p[1, 3] * f11),
            )
            i0 = lax.rsqrt(p[0, 0])
            l10, l20, l30 = p[0, 1] * i0, p[0, 2] * i0, p[0, 3] * i0
            i1 = lax.rsqrt(p[1, 1] - l10 * l10)
            l21, l31 = (p[1, 2] - l20 * l10) * i1, (p[1, 3] - l30 * l10) * i1
            i2 = lax.rsqrt(p[2, 2] - (l20 * l20 + l21 * l21))
            l32 = (p[2, 3] - (l30 * l20 + l31 * l21)) * i2
            i3 = lax.rsqrt(p[3, 3] - (l30 * l30 + l31 * l31 + l32 * l32))
            solved = []
            for group, target in ((rows, done_main), (more, done_extra)):
                if group is None:
                    solved.append(None)
                    continue
                u2 = group[2] - (f00 * group[0] + f10 * group[1])
                u3 = group[3] - (f01 * group[0] + f11 * group[1])
                z2 = g00 * u2 + g01 * u3
                z3 = g01 * u2 + g11 * u3
                z0 = (e00 * group[0] + e01 * group[1]) - (f00 * z2 + f01 * z3)
                z1 = (e01 * group[0] + e11 * group[1]) - (f10 * z2 + f11 * z3)
                solved.append((z0, z1, z2, z3))
                r0 = group[0] * i0
                r1 = (group[1] - l10 * r0) * i1
                r2 = (group[2] - (l20 * r0 + l21 * r1)) * i2
                r3 = (group[3] - (l30 * r0 + l31 * r1 + l32 * r2)) * i3
                quad = jnp.where(
                    line == first,
                    r0,
                    jnp.where(line == first + 1, r1, jnp.where(line == first + 2, r2, r3)),
                )
                target[tile] = quad if first == 0 else jnp.where(line < 4, target[tile], quad)
            for j in range(tile if first == 0 else tile + 1, tiles):
                weights = [spread(main[j][:, at + i : at + i + 1]) for i in range(4)]
                if j == tile:
                    weights = [jnp.where(line >= 4, weight, 0.0) for weight in weights]
                base = jnp.where(inside, 0.0, main[j]) if job["inverse"] else main[j]
                z = solved[0]
                main[j] = base - (
                    (weights[0] * z[0] + weights[1] * z[1]) + (weights[2] * z[2] + weights[3] * z[3])
                )
                if extra:
                    z = solved[1]
                    extra[j] = extra[j] - (
                        (weights[0] * z[0] + weights[1] * z[1]) + (weights[2] * z[2] + weights[3] * z[3])
                    )
    row = lax.broadcasted_iota(jnp.int32, (HALF, HALF), 0)
    col = lax.broadcasted_iota(jnp.int32, (HALF, HALF), 1)
    results = []
    for job, (done_main, done_extra) in zip(jobs, done):
        main = jnp.concatenate(done_main, 0)
        keep = (col <= row) if job["inverse"] else (col >= row)
        main = jnp.where(keep, main, 0.0)
        results.append((main, jnp.concatenate(done_extra, 0) if job["extra"] else None))
    return results


def tiles_of(matrix):
    return [matrix[8 * i : 8 * i + 8, :] for i in range(HALF // 8)]


def factors(packed_ref, pivot_ref, weights_ref, offset_ref, factor_ref):
    channels = 2 * HALF
    base = 6 * HALF
    line0 = packed_ref[base : base + 8, :]
    number = jnp.broadcast_to(line0[2:3, 0:1], (1, HALF))
    pairs = jnp.broadcast_to(line0[3:4, 0:1], (1, HALF))
    noise_scale = 1.0 / (2.0 * pairs)
    scale = 1.0 / number
    mean0, mean1 = line0[0:1] * scale, line0[1:2] * scale
    column0 = as_column(mean0)
    column1 = as_column(mean1)
    part = lambda i: packed_ref[HALF * i : HALF * (i + 1), :]
    n00, n01, n11 = part(0) * noise_scale, part(1) * noise_scale, part(2) * noise_scale
    s00 = part(3) * scale - column0 * mean0
    s01 = part(4) * scale - column0 * mean1
    s11 = part(5) * scale - column1 * mean1
    (w00, y), (k00, k01) = eliminate(
        [
            dict(main=tiles_of(n00), extra=tiles_of(n01), inverse=True),
            dict(main=tiles_of(s00), extra=tiles_of(s01), inverse=False),
        ]
    )
    n11 = n11 - exact(y, y, 0, 0)
    s11 = s11 - exact(k01, k01, 0, 0)
    (w11, _), (k11, _) = eliminate(
        [
            dict(main=tiles_of(n11), extra=None, inverse=True),
            dict(main=tiles_of(s11), extra=None, inverse=False),
        ]
    )
    w10 = -exact(w11, exact(y, w00, 0, 0))
    factor_ref[:HALF, :HALF] = exact(k00, w00, 1, 1)
    factor_ref[:HALF, HALF:] = exact(k00, w10, 1, 1) + exact(k01, w11, 1, 1)
    factor_ref[HALF:, :HALF] = jnp.zeros((HALF, HALF), F32)
    factor_ref[HALF:, HALF:] = exact(k11, w11, 1, 1)
    mean0 = jnp.broadcast_to(mean0, (8, HALF)) - pivot_ref[:, :HALF]
    mean1 = jnp.broadcast_to(mean1, (8, HALF)) - pivot_ref[:, HALF:]
    offset_ref[:, :HALF] = exact(mean0, w00, 1, 1)
    offset_ref[:, HALF:] = exact(mean0, w10, 1, 1) + exact(mean1, w11, 1, 1)
    left = jnp.concatenate([jnp.transpose(w00), jnp.zeros((HALF, HALF), F32)], 0)
    right = jnp.concatenate([jnp.transpose(w10), jnp.transpose(w11)], 0)
    high, low = split(jnp.concatenate([left, right], 1))
    weights_ref[0:channels, :] = high
    weights_ref[channels : 2 * channels, :] = low
    weights_ref[2 * channels :, :] = high


def whiten_rows(high, low, weights):
    return jnp.dot(jnp.concatenate([high, high, low], 1), weights, preferred_element_type=F32)


def whiten_kernel(
    packed_ref,
    pivot_ref,
    high_from,
    low_from,
    valid_ref,
    below_ref,
    right_ref,
    white_ref,
    noise_ref,
    factor_ref,
    high_ref,
    low_ref,
    weights_ref,
    offset_ref,
    plain,
    right_edge,
    neighbours,
    arrived,
):
    step = pl.program_id(0)
    steps = pl.num_programs(0)
    rows, cols = valid_ref.shape
    channels = high_ref.shape[2]

    @pl.when(step == 0)
    def _():
        valid = valid_ref[...].astype(F32)
        down = jnp.concatenate([valid[1:], below_ref[cols : cols + 1, :]], 0)
        right = jnp.concatenate([valid[:, 1:], right_ref[:, channels : channels + 1]], 1)
        neighbours[...] = down + right
        copies = [
            pltpu.make_async_copy(high_from, high_ref, arrived.at[0]),
            pltpu.make_async_copy(low_from, low_ref, arrived.at[1]),
        ]
        for copy in copies:
            copy.start()
        factors(packed_ref, pivot_ref, weights_ref, offset_ref, factor_ref)
        pivot = pivot_ref[0:1, :]
        below = below_ref[0:cols, :] - as_column(below_ref[cols : cols + 1, :]) * pivot
        plain[STEP_ROWS * (cols + 8) :, :] = whiten_rows(*split(below), weights_ref[...])
        right = right_ref[:, :channels] - right_ref[:, channels : channels + 1] * pivot
        right_edge[...] = whiten_rows(*split(right), weights_ref[...])
        for copy in copies:
            copy.wait()

    start = pl.multiple_of((steps - 1 - step) * STEP_ROWS, STEP_ROWS)
    valid = jnp.transpose(valid_ref[pl.ds(start, STEP_ROWS), :].astype(F32))
    number = jnp.transpose(neighbours[pl.ds(start, STEP_ROWS), :])
    edge = right_edge[pl.ds(start, STEP_ROWS), :]
    offset = offset_ref[0:1, :]
    weights = weights_ref[...]
    for row in reversed(range(STEP_ROWS)):
        base = row * (cols + 8)
        plain[base : base + cols, :] = whiten_rows(high_ref[start + row], low_ref[start + row], weights)
        plain[base + cols : base + cols + 1, :] = edge[row : row + 1]
        for at in range(0, cols, CHUNK):
            here = plain[base + at : base + at + CHUNK, :]
            right = plain[base + at + 1 : base + at + 1 + CHUNK, :]
            below = plain[base + cols + 8 + at : base + cols + 8 + at + CHUNK, :]
            ok = valid[at : at + CHUNK, row : row + 1]
            white_ref[row, at : at + CHUNK, :] = (here - ok * offset).astype(BF16)
            around = number[at : at + CHUNK, row : row + 1]
            noise_ref[row, at : at + CHUNK, :] = (ok * (below + right) - around * here).astype(BF16)
    plain[STEP_ROWS * (cols + 8) :, :] = plain[0 : cols, :]


def whiten(packed, pivot, high, low, good_pixels, below, right):
    rows, cols, channels = high.shape
    steps = rows // STEP_ROWS
    pixels = rows * cols
    whole = lambda shape: pl.BlockSpec(shape, lambda i: (0,) * len(shape))
    block = pl.BlockSpec((STEP_ROWS, cols, channels), lambda i: (steps - 1 - i, 0, 0))
    return pl.pallas_call(
        whiten_kernel,
        grid=(steps,),
        in_specs=[
            whole(packed.shape),
            whole(pivot.shape),
            pl.BlockSpec(memory_space=pl.ANY),
            pl.BlockSpec(memory_space=pl.ANY),
            whole((rows, cols)),
            whole(below.shape),
            whole(right.shape),
        ],
        out_specs=[block, block, whole((channels, channels))],
        out_shape=[jax.ShapeDtypeStruct(high.shape, BF16)] * 2 + [jax.ShapeDtypeStruct((channels, channels), F32)],
        scratch_shapes=[
            pltpu.VMEM(high.shape, BF16),
            pltpu.VMEM(low.shape, BF16),
            pltpu.VMEM((3 * channels, channels), BF16),
            pltpu.VMEM((8, channels), F32),
            pltpu.VMEM((STEP_ROWS * (cols + 8) + cols, channels), F32),
            pltpu.VMEM((rows, channels), F32),
            pltpu.VMEM((rows, cols), F32),
            pltpu.SemaphoreType.DMA((2,)),
        ],
        compiler_params=pltpu.CompilerParams(vmem_limit_bytes=48 * 1024 * 1024),
        cost_estimate=pl.CostEstimate(
            flops=6 * pixels * channels * channels, bytes_accessed=8 * pixels * channels, transcendentals=0
        ),
        name="whiten",
    )(packed, pivot, high, low, good_pixels, below, right)


def from_next(value, axis):
    count = lax.axis_size(axis)
    return lax.ppermute(value, axis, [(source, source - 1) for source in range(1, count)])


def summed(packed, axes):
    devices = lax.axis_size(axes)
    share = packed.reshape(devices, packed.shape[0] // devices, HALF)
    mine = jnp.sum(lax.all_to_all(share, axes, 0, 0), 0)
    every = lax.all_to_all(jnp.broadcast_to(mine[None], share.shape), axes, 0, 0)
    return every.reshape(packed.shape)


def on_device(raw_counts, gain_class, good_pixels, class_gains):
    axes = ("col", "row")
    raw_counts = pltpu.with_memory_space_constraint(raw_counts, pltpu.HBM)
    first_row, first_col = edges(raw_counts, gain_class, good_pixels, class_gains)
    below = from_next(first_row, "row")
    right = from_next(first_col, "col")
    high, low, products, sums, pivot = moments(raw_counts, gain_class, good_pixels, class_gains)
    high, low = (pltpu.with_memory_space_constraint(part, pltpu.HBM) for part in (high, low))
    devices = lax.axis_size(axes)
    length = -(-(6 * HALF + 8) // (8 * devices)) * 8 * devices
    packed = pack(products, sums, pivot, below, right, high, low, good_pixels, length)
    return whiten(summed(packed, axes), pivot, high, low, good_pixels, below, right)


def solution(mesh):
    return jax.shard_map(
        on_device,
        mesh=mesh,
        in_specs=(P("row", "col", None), P("row", "col"), P("row", "col"), P()),
        out_specs=(P("row", "col", None), P("row", "col", None), P()),
        check_vma=False,
    )
```

time: 617 us -> 96.1 us (0.16); the launches traced: 609 us -> 95.8 us
  waiting for transfers between devices: 233 us -> 0.01 us
  other arithmetic: 129 us -> 0.14 us
  matrix products: 126 us -> 0 us
  Pallas kernels: 0 us -> 47.2 us
  blocking collectives: 71 us -> 43 us
  local copies, waits for them, and re-layouts: 23.3 us -> 0.05 us
  between operations: 19.2 us -> 0.87 us
    psum x2 -> x0, waiting for transfers between devices: 232 us -> none  [the longest x1 122 us: on_device(): gram_sum = lax.psum(gram_local, ('col', 'row'))]
    dot_general x6 -> x0, matrix products: 124 us -> none  [the longest x3 85.6 us: products(): lax.dot_general(left, right, (((0,), (0,)), ((), ())), precision=lax.Prec...]
    another operation x16 -> x0, other arithmetic: 88.5 us -> none  [the longest x7 34.7 us: on_device(): factor = jnp.linalg.cholesky(gram_sum / count).T]
    psum x1 -> x0, blocking collectives: 71 us -> none  [on_device(): lax.psum((noise_local, pixel_sum, jnp.sum(valid), jnp.sum(down_w) + jnp.s...]
    pallas_call x0 -> x4, Pallas kernels: none -> 47.2 us  [the longest x1 24.4 us: whiten(): pl.pallas_call(whiten_kernel, grid=(steps,), in_specs=[whole(packed.shape...]
    all_to_all x0 -> x2, blocking collectives: none -> 43 us  [the longest x1 24.9 us: summed(): mine = jnp.sum(lax.all_to_all(share, axes, 0, 0), 0)]
    add x1 -> x0, other arithmetic: 27.7 us -> none  [on_device(): flat_down + flat_right]
    slice x8 -> x0, local copies, waits for them, and re-layouts: 13.8 us -> none  [the longest x1 7.26 us: on_device(): right_next = jnp.concatenate([calibrated[:, 1:], right_vals], 1)]
  transfers between devices with their start and end apart: 6 -> 2, of which waited for: 2 -> 0; matrix products, arithmetic and copies ran while one was open for 18% -> 0% of each run, Pallas kernels for 0% -> 19%
where the time goes in v1:
time: 96.1 us; the launch traced here: 95.8 us
  Pallas kernels  47.2 us (49%)
  blocking collectives  43 us (45%)
  starting transfers between devices  4.61 us (5%)
    all_to_all x1, blocking collectives, summed(): mine = jnp.sum(lax.all_to_all(share, axes, 0, 0), 0)  24.9 us
    pallas_call x1, Pallas kernels, whiten(): pl.pallas_call(whiten_kernel, grid=(steps,), in_specs=[whole(packed.shape...  24.4 us
    pallas_call x1, Pallas kernels, moments(): pl.pallas_call(moments_kernel, grid=(rows // STEP_ROWS,), in_specs=[block...  18.4 us
    all_to_all x1, blocking collectives, summed(): lax.all_to_all(jnp.broadcast_to(mine[None], share.shape), axes, 0, 0)  18.1 us
    ppermute x2, starting transfers between devices, from_next(): lax.ppermute(value, axis, [(source, source - 1) for source in range(1, co...  4.61 us
    pallas_call x1, Pallas kernels, pack(): pl.pallas_call(pack_kernel, grid=(1,), in_specs=[whole(products.shape), w...  2.26 us
    pallas_call x1, Pallas kernels, edges(): pl.pallas_call(edges_kernel, grid=(1,), in_specs=[whole((1, cols, channel...  2.12 us
  transfers between devices with their start and end apart: 2, of which 0 were waited for; matrix products, arithmetic and copies ran while one was open for 0% of the time, Pallas kernels for 19%

profile of v1, /device:TPU:1, one launch (start us, length us, event | category | flops | bytes accessed | tf_op | source)
XLA Modules:
  0.0 95.8 jit_solution(11327345720958861844)
XLA Ops:
  0.6 0.0 copy-start
  0.6 0.0 copy-start.2
  0.7 0.0 copy-start.1
  0.7 2.1 %edges.1 = (f32[264,256]{1,0:T(8,128)}, f32[64,384]{1,0:T(8,128)}) custom-call(bf16[64,256,256]{2,1,0:T(8,128)(2,1)} %col_ref.1, bf16[64,256,256]{2,1,0:T(8,128)(2,1)} %col_ref.1, s32[64,256]{1,0:T(8,128)} %class_ref.3, s32[64,256]{1,0:T(8,128)} %valid_ref.7, f32[16,256]{1,0:T(8,128)} %gains_ref.3), custom_call_target="tpu_custom_call" | custom-call | tf_op jit(solution)/shard_map/edges/pallas_call | solution.py:74
  2.8 1.3 %collective-permute-start.1 = (f32[64,384]{1,0:T(8,128)}, f32[64,384]{1,0:T(8,128)S(1)}, u32[]{:S(2)}, u32[]{:S(2)}) collective-permute-start(f32[64,384]{1,0:T(8,128)} %get-tuple-element.14), channel_id=1, source_target_pairs={{8,0},{16,8},{24,16},{32,24},{40,32},{48,40},{56,48},{64,56},{72,6... | collective-permute-start | bytes 294920 | tf_op jit(solution)/shard_map/ppermute | solution.py:496
  4.1 3.3 %collective-permute-start = (f32[264,256]{1,0:T(8,128)}, f32[264,256]{1,0:T(8,128)S(1)}, u32[]{:S(2)}, u32[]{:S(2)}) collective-permute-start(f32[264,256]{1,0:T(8,128)} %get-tuple-element.13), channel_id=1, source_target_pairs={{1,0},{2,1},{3,2},{4,3},{5,4},{6,5},{7,6},{9,8},{10,9},{11,10},{12... | collective-permute-start | bytes 811016 | tf_op jit(solution)/shard_map/ppermute | solution.py:496
  7.4 0.0 copy-done
  7.4 0.0 copy-done.2
  7.4 0.0 copy-done.1
  7.4 18.4 %moments.1 = (bf16[64,256,256]{2,1,0:T(8,128)(2,1)}, bf16[64,256,256]{2,1,0:T(8,128)(2,1)}, f32[256,512]{1,0:T(8,128)S(1)}, f32[8,256]{1,0:T(8,128)S(1)}, f32[8,256]{1,0:T(8,128)S(1)}) custom-call(bf16[64,256,256]{2,1,0:T(8,128)(2,1)} %col_ref.1, s32[64,256]{1,0:T(8,128)S(1)} %copy-done.1, s32[64,256]{1,0:T(8,128)S(1)} %copy-done, f32[16,256]{1,0:T(8,128)S(1)} %copy-done.2), custom_call_target="tpu_custom_call" | custom-call | flops 10737418240 | bytes 25165824 | tf_op jit(solution)/shard_map/moments/pallas_call | solution.py:151
  25.8 0.0 collective-permute-done.1.right_ref
  25.8 0.0 collective-permute-done.below_ref
  25.9 2.3 %pack.1 = f32[1024,128]{1,0:T(8,128)S(1)} custom-call(f32[256,512]{1,0:T(8,128)S(1)} %get-tuple-element.10.products_ref, f32[8,256]{1,0:T(8,128)S(1)} %get-tuple-element.11.sums_ref, f32[8,256]{1,0:T(8,128)S(1)} %get-tuple-element.12.pivot_ref, f32[264,256]{1,0:T(8,128)S(1)} %collective-permute-done.below_ref, ...), custom_call_target="tpu_custom_call" | custom-call | tf_op jit(solution)/shard_map/pack/pallas_call | solution.py:223
  28.1 24.9 %all_to_all.10 = f32[128,8,128]{2,1,0:T(8,128)S(1)} all-to-all(f32[128,8,128]{2,1,0:T(8,128)S(1)} %bitcast.2), channel_id=1, replica_groups=mesh['col'=16,'row'=8] {'col','row'}, dimensions={0} | all-to-all | bytes 1048576 | tf_op jit(solution)/shard_map/all_to_all | solution.py:502
  53.0 0.1 reduce_sum.9
  53.2 18.1 %all_to_all.11 = f32[128,8,128]{2,1,0:T(8,128)S(1)} all-to-all(f32[128,8,128]{2,1,0:T(8,128)S(1)} %broadcast_in_dim.2), channel_id=1, replica_groups=mesh['col'=16,'row'=8] {'col','row'}, dimensions={0} | all-to-all | bytes 1048576 | tf_op jit(solution)/shard_map/all_to_all | solution.py:503
  71.3 24.4 %whiten.1 = (bf16[64,256,256]{2,1,0:T(8,128)(2,1)}, bf16[64,256,256]{2,1,0:T(8,128)(2,1)}, f32[256,256]{1,0:T(8,128)}) custom-call(f32[1024,128]{1,0:T(8,128)S(1)} %bitcast.3, f32[8,256]{1,0:T(8,128)S(1)} %get-tuple-element.12.pivot_ref, bf16[64,256,256]{2,1,0:T(8,128)(2,1)} %get-tuple-element.15.high_row.high_col.high_from, ...), custom_call_target="tpu_custom_call" | custom-call | flops 6442450944 | bytes 33554432 | tf_op jit(solution)/shard_map/whiten/pallas_call | solution.py:462
  (1 shorter events, 0.0 us)
Async XLA Ops:
  0.6 6.8 %copy-start = (s32[64,256]{1,0:T(8,128)S(1)}, s32[64,256]{1,0:T(8,128)}, u32[]{:S(2)}) copy-start(s32[64,256]{1,0:T(8,128)} %valid_ref.7) | copy-start | bytes 196612
  0.6 6.8 %copy-start.2 = (f32[16,256]{1,0:T(8,128)S(1)}, f32[16,256]{1,0:T(8,128)}, u32[]{:S(2)}) copy-start(f32[16,256]{1,0:T(8,128)} %gains_ref.3) | copy-start | bytes 49156
  0.7 6.8 %copy-start.1 = (s32[64,256]{1,0:T(8,128)S(1)}, s32[64,256]{1,0:T(8,128)}, u32[]{:S(2)}) copy-start(s32[64,256]{1,0:T(8,128)} %class_ref.3) | copy-start | bytes 196612
  2.8 23.1 %collective-permute-start.1 = (f32[64,384]{1,0:T(8,128)}, f32[64,384]{1,0:T(8,128)S(1)}, u32[]{:S(2)}, u32[]{:S(2)}) collective-permute-start(f32[64,384]{1,0:T(8,128)} %get-tuple-element.14), channel_id=1, source_target_pairs={{8,0},{16,8},{24,16},{32,24},{40,32},{48,40},{56,48},{64,56},{72,6... | collective-permute-start | bytes 294920 | tf_op jit(solution)/shard_map/ppermute | solution.py:496
  4.1 21.8 %collective-permute-start = (f32[264,256]{1,0:T(8,128)}, f32[264,256]{1,0:T(8,128)S(1)}, u32[]{:S(2)}, u32[]{:S(2)}) collective-permute-start(f32[264,256]{1,0:T(8,128)} %get-tuple-element.13), channel_id=1, source_target_pairs={{1,0},{2,1},{3,2},{4,3},{5,4},{6,5},{7,6},{9,8},{10,9},{11,10},{12... | collective-permute-start | bytes 811016 | tf_op jit(solution)/shard_map/ppermute | solution.py:496

commit v2 on v1

--- a/solution.py
+++ b/solution.py
@@ -5,7 +5,7 @@
 from jax.experimental.pallas import tpu as pltpu
 from jax.sharding import PartitionSpec as P
 
-STEP_ROWS = 8
+STEP_ROWS = 16
 CHUNK = 32
 HALF = 128
 HIGHEST = lax.Precision.HIGHEST
@@ -198,11 +198,15 @@
     shift = total + number * pivot
     second = products_ref[:, channels:] + (as_column(pivot) * shift + as_column(total) * pivot)
     total = shift
+    row = lax.broadcasted_iota(jnp.int32, (HALF, HALF), 0)
+    col = lax.broadcasted_iota(jnp.int32, (HALF, HALF), 1)
     at = 0
+    diagonals = []
     for matrix in (noise, second):
-        for part in (matrix[:HALF, :HALF], matrix[:HALF, HALF:], matrix[HALF:, HALF:]):
-            packed_ref[at : at + HALF, :] = part
-            at += HALF
+        packed_ref[at : at + HALF, :] = jnp.where(col <= row, matrix[:HALF, :HALF], matrix[HALF:, HALF:])
+        packed_ref[at + HALF : at + 2 * HALF, :] = matrix[:HALF, HALF:]
+        diagonals.append(jnp.sum(jnp.where(row == col, matrix[HALF:, HALF:], 0.0), 0, keepdims=True))
+        at += 2 * HALF
     pairs = jnp.sum(valid[1:] * valid[:-1], keepdims=True) + jnp.sum(valid[:, 1:] * valid[:, :-1], keepdims=True)
     pairs = pairs + jnp.sum(valid[rows - 1 :] * below_row, keepdims=True)
     pairs = pairs + jnp.sum(last_col * right_valid, keepdims=True)
@@ -210,9 +214,20 @@
     packed_ref[at : at + 8, :] = jnp.where(
         line == 0,
         total[:, :HALF],
-        jnp.where(line == 1, total[:, HALF:], jnp.where(line == 2, number, jnp.where(line == 3, pairs, 0.0))),
+        jnp.where(
+            line == 1,
+            total[:, HALF:],
+            jnp.where(
+                line == 2,
+                number,
+                jnp.where(
+                    line == 3, pairs, jnp.where(line == 4, diagonals[0], jnp.where(line == 5, diagonals[1], 0.0))
+                ),
+            ),
+        ),
     )
-    packed_ref[at + 8 :, :] = jnp.zeros((packed_ref.shape[0] - at - 8, HALF), F32)
+    if packed_ref.shape[0] > at + 8:
+        packed_ref[at + 8 :, :] = jnp.zeros((packed_ref.shape[0] - at - 8, HALF), F32)
 
 
 def pack(products, sums, pivot, below, right, high, low, good_pixels, length):
@@ -337,7 +352,7 @@
 
 def factors(packed_ref, pivot_ref, weights_ref, offset_ref, factor_ref):
     channels = 2 * HALF
-    base = 6 * HALF
+    base = 4 * HALF
     line0 = packed_ref[base : base + 8, :]
     number = jnp.broadcast_to(line0[2:3, 0:1], (1, HALF))
     pairs = jnp.broadcast_to(line0[3:4, 0:1], (1, HALF))
@@ -347,10 +362,21 @@
     column0 = as_column(mean0)
     column1 = as_column(mean1)
     part = lambda i: packed_ref[HALF * i : HALF * (i + 1), :]
-    n00, n01, n11 = part(0) * noise_scale, part(1) * noise_scale, part(2) * noise_scale
-    s00 = part(3) * scale - column0 * mean0
-    s01 = part(4) * scale - column0 * mean1
-    s11 = part(5) * scale - column1 * mean1
+    row = lax.broadcasted_iota(jnp.int32, (HALF, HALF), 0)
+    col = lax.broadcasted_iota(jnp.int32, (HALF, HALF), 1)
+
+    def diagonal_blocks(block, diagonal):
+        turned = jnp.transpose(block)
+        lower = jnp.where(col <= row, block, turned)
+        upper = jnp.where(col > row, block, turned)
+        return lower, jnp.where(col == row, diagonal, upper)
+
+    n00, n11 = (block * noise_scale for block in diagonal_blocks(part(0), line0[4:5]))
+    n01 = part(1) * noise_scale
+    s00, s11 = diagonal_blocks(part(2), line0[5:6])
+    s00 = s00 * scale - column0 * mean0
+    s01 = part(3) * scale - column0 * mean1
+    s11 = s11 * scale - column1 * mean1
     (w00, y), (k00, k01) = eliminate(
         [
             dict(main=tiles_of(n00), extra=tiles_of(n01), inverse=True),
@@ -496,26 +522,35 @@
     return lax.ppermute(value, axis, [(source, source - 1) for source in range(1, count)])
 
 
-def summed(packed, axes):
-    devices = lax.axis_size(axes)
-    share = packed.reshape(devices, packed.shape[0] // devices, HALF)
-    mine = jnp.sum(lax.all_to_all(share, axes, 0, 0), 0)
-    every = lax.all_to_all(jnp.broadcast_to(mine[None], share.shape), axes, 0, 0)
-    return every.reshape(packed.shape)
+def summed(packed):
+    axes = ("col", "row")
+    cols, rows = (lax.axis_size(axis) for axis in axes)
+    core = lax.axis_index("row") % 2
+    swap = [(i, i ^ 1) for i in range(rows)]
+    groups = [[c * rows + r for c in range(cols) for r in range(k, rows, 2)] for k in range(2)]
+    peers = cols * rows // 2
+    parts = packed.reshape(2, packed.shape[0] // 2, HALF)
+    kept = lax.dynamic_index_in_dim(parts, core, 0, keepdims=False)
+    given = lax.dynamic_index_in_dim(parts, 1 - core, 0, keepdims=False)
+    share = (kept + lax.ppermute(given, "row", swap)).reshape(peers, -1, 1, HALF)
+    mine = jnp.sum(lax.all_to_all(share, axes, 0, 0, axis_index_groups=groups), 0)
+    every = lax.all_to_all(jnp.broadcast_to(mine[None], share.shape), axes, 0, 0, axis_index_groups=groups)
+    every = every.reshape(kept.shape)
+    other = lax.ppermute(every, "row", swap)
+    return jnp.concatenate([jnp.where(core == 0, every, other), jnp.where(core == 0, other, every)], 0)
 
 
 def on_device(raw_counts, gain_class, good_pixels, class_gains):
-    axes = ("col", "row")
     raw_counts = pltpu.with_memory_space_constraint(raw_counts, pltpu.HBM)
     first_row, first_col = edges(raw_counts, gain_class, good_pixels, class_gains)
     below = from_next(first_row, "row")
     right = from_next(first_col, "col")
     high, low, products, sums, pivot = moments(raw_counts, gain_class, good_pixels, class_gains)
     high, low = (pltpu.with_memory_space_constraint(part, pltpu.HBM) for part in (high, low))
-    devices = lax.axis_size(axes)
-    length = -(-(6 * HALF + 8) // (8 * devices)) * 8 * devices
+    devices = lax.axis_size(("col", "row"))
+    length = -(-(4 * HALF + 8) // devices) * devices
     packed = pack(products, sums, pivot, below, right, high, low, good_pixels, length)
-    return whiten(summed(packed, axes), pivot, high, low, good_pixels, below, right)
+    return whiten(summed(packed), pivot, high, low, good_pixels, below, right)
 
 
 def solution(mesh):

time: 96.1 us -> 92.3 us (0.960)
  blocking collectives: 43 us -> 34.7 us
  starting transfers between devices: 4.61 us -> 7.38 us
  waiting for transfers between devices: 0.01 us -> 2.41 us
    all_to_all x2, blocking collectives: 43 us -> 34.7 us  [the longest x1 21 us: summed(): lax.all_to_all(share, axes, 0, 0, axis_index_groups=groups)]
    ppermute x0 -> x2, starting transfers between devices: none -> 2.77 us  [the longest x1 2.68 us: summed(): other = lax.ppermute(every, 'row', swap)]
    ppermute x0 -> x2, waiting for transfers between devices: none -> 2.4 us  [the longest x1 1.37 us: summed(): lax.ppermute(given, 'row', swap)]
  transfers between devices with their start and end apart: 2 -> 4, of which waited for: 0 -> 2; matrix products, arithmetic and copies ran while one was open for 0% -> 0% of each run, Pallas kernels for 19% -> 19%
where the time goes in v2:
time: 92.3 us; the launch traced here: 92 us
  Pallas kernels  46.3 us (50%)
  blocking collectives  34.7 us (38%)
  starting transfers between devices  7.38 us (8%)
  waiting for transfers between devices  2.41 us (3%)
    pallas_call x1, Pallas kernels, whiten(): pl.pallas_call(whiten_kernel, grid=(steps,), in_specs=[whole(packed.shape...  24.1 us
    all_to_all x1, blocking collectives, summed(): lax.all_to_all(share, axes, 0, 0, axis_index_groups=groups)  21 us
    pallas_call x1, Pallas kernels, moments(): pl.pallas_call(moments_kernel, grid=(rows // STEP_ROWS,), in_specs=[block...  17.8 us
    all_to_all x1, blocking collectives, summed(): lax.all_to_all(jnp.broadcast_to(mine[None], share.shape), axes, 0, 0, axi...  13.7 us
    ppermute x2, starting transfers between devices, from_next(): lax.ppermute(value, axis, [(source, source - 1) for source in range(1, co...  4.61 us
    ppermute x1, starting transfers between devices, summed(): other = lax.ppermute(every, 'row', swap)  2.68 us
    pallas_call x1, Pallas kernels, pack(): pl.pallas_call(pack_kernel, grid=(1,), in_specs=[whole(products.shape), w...  2.27 us
    pallas_call x1, Pallas kernels, edges(): pl.pallas_call(edges_kernel, grid=(1,), in_specs=[whole((1, cols, channel...  2.12 us
  transfers between devices with their start and end apart: 4, of which 2 were waited for; matrix products, arithmetic and copies ran while one was open for 0% of the time, Pallas kernels for 19%

profile of v2, /device:TPU:1, one launch (start us, length us, event | category | flops | bytes accessed | tf_op | source)
XLA Modules:
  0.0 92.0 jit_solution(13258837383065707132)
XLA Ops:
  0.6 0.0 copy-start
  0.6 0.0 copy-start.2
  0.7 0.0 copy-start.1
  0.7 2.1 %edges.1 = (f32[264,256]{1,0:T(8,128)}, f32[64,384]{1,0:T(8,128)}) custom-call(bf16[64,256,256]{2,1,0:T(8,128)(2,1)} %col_ref.1, bf16[64,256,256]{2,1,0:T(8,128)(2,1)} %col_ref.1, s32[64,256]{1,0:T(8,128)} %class_ref.3, s32[64,256]{1,0:T(8,128)} %valid_ref.7, f32[16,256]{1,0:T(8,128)} %gains_ref.3), custom_call_target="tpu_custom_call" | custom-call | tf_op jit(solution)/shard_map/edges/pallas_call | solution.py:74
  2.8 1.3 %collective-permute-start.1 = (f32[64,384]{1,0:T(8,128)}, f32[64,384]{1,0:T(8,128)S(1)}, u32[]{:S(2)}, u32[]{:S(2)}) collective-permute-start(f32[64,384]{1,0:T(8,128)} %get-tuple-element.14), channel_id=1, source_target_pairs={{8,0},{16,8},{24,16},{32,24},{40,32},{48,40},{56,48},{64,56},{72,6... | collective-permute-start | bytes 294920 | tf_op jit(solution)/shard_map/ppermute | solution.py:522
  4.1 3.3 %collective-permute-start = (f32[264,256]{1,0:T(8,128)}, f32[264,256]{1,0:T(8,128)S(1)}, u32[]{:S(2)}, u32[]{:S(2)}) collective-permute-start(f32[264,256]{1,0:T(8,128)} %get-tuple-element.13), channel_id=1, source_target_pairs={{1,0},{2,1},{3,2},{4,3},{5,4},{6,5},{7,6},{9,8},{10,9},{11,10},{12... | collective-permute-start | bytes 811016 | tf_op jit(solution)/shard_map/ppermute | solution.py:522
  7.4 0.0 copy-done
  7.4 0.0 copy-done.2
  7.4 0.0 copy-done.1
  7.4 17.8 %moments.1 = (bf16[64,256,256]{2,1,0:T(8,128)(2,1)}, bf16[64,256,256]{2,1,0:T(8,128)(2,1)}, f32[256,512]{1,0:T(8,128)S(1)}, f32[8,256]{1,0:T(8,128)S(1)}, f32[8,256]{1,0:T(8,128)S(1)}) custom-call(bf16[64,256,256]{2,1,0:T(8,128)(2,1)} %col_ref.1, s32[64,256]{1,0:T(8,128)S(1)} %copy-done.1, s32[64,256]{1,0:T(8,128)S(1)} %copy-done, f32[16,256]{1,0:T(8,128)S(1)} %copy-done.2), custom_call_target="tpu_custom_call" | custom-call | flops 10737418240 | bytes 25165824 | tf_op jit(solution)/shard_map/moments/pallas_call | solution.py:151
  25.3 0.0 collective-permute-done.1.right_ref
  25.3 0.0 collective-permute-done.below_ref
  25.3 2.3 %pack.1 = f32[640,128]{1,0:T(8,128)S(1)} custom-call(f32[256,512]{1,0:T(8,128)S(1)} %get-tuple-element.10.products_ref, f32[8,256]{1,0:T(8,128)S(1)} %get-tuple-element.11.sums_ref, f32[8,256]{1,0:T(8,128)S(1)} %get-tuple-element.12.pivot_ref, f32[264,256]{1,0:T(8,128)S(1)} %collective-permute-done.below_ref, ...), custom_call_target="tpu_custom_call" | custom-call | tf_op jit(solution)/shard_map/pack/pallas_call | solution.py:238
  27.6 0.1 collective-permute-start.2
  27.7 1.4 %collective-permute-done.2 = f32[320,128]{1,0:T(8,128)S(1)} collective-permute-done((f32[320,128]{1,0:T(8,128)S(1)}, f32[320,128]{1,0:T(8,128)S(1)}, u32[]{:S(2)}, u32[]{:S(2)}) %collective-permute-start.2) | collective-permute-done | bytes 163872 | tf_op jit(solution)/shard_map/ppermute | solution.py:535
  29.1 21.0 %all_to_all.10 = f32[64,5,1,128]{3,2,1,0:T(1,128)S(1)} all-to-all(f32[64,5,1,128]{3,2,1,0:T(1,128)S(1)} %bitcast.9), channel_id=1, replica_groups={{0,2,4,6,8,10,12,14,16,18,20,22,24,26,28,30,32,34,36,38,40,42,44,46,48,..., dimensions={0} | all-to-all | bytes 327680 | tf_op jit(solution)/shard_map/all_to_all | solution.py:536
  50.1 0.1 reduce_sum.9
  50.2 0.1 broadcast_in_dim.2
  50.3 13.7 %all_to_all.11 = f32[64,5,1,128]{3,2,1,0:T(1,128)S(1)} all-to-all(f32[64,5,1,128]{3,2,1,0:T(1,128)S(1)} %broadcast_in_dim.2), channel_id=1, replica_groups={{0,2,4,6,8,10,12,14,16,18,20,22,24,26,28,30,32,34,36,38,40,42,44,46,48,..., dimensions={0} | all-to-all | bytes 327680 | tf_op jit(solution)/shard_map/all_to_all | solution.py:537
  64.0 2.7 %collective-permute-start.3 = (f32[320,128]{1,0:T(8,128)S(1)}, f32[320,128]{1,0:T(8,128)S(1)}, u32[]{:S(2)}, u32[]{:S(2)}) collective-permute-start(f32[320,128]{1,0:T(8,128)S(1)} %bitcast.10), channel_id=1, source_target_pairs={{0,1},{1,0},{2,3},{3,2},{4,5},{5,4},{6,7},{7,6},{8,9},{9,8},{10,11... | collective-permute-start | bytes 491528 | tf_op jit(solution)/shard_map/ppermute | solution.py:539
  66.7 1.0 %collective-permute-done.3 = f32[320,128]{1,0:T(8,128)S(1)} collective-permute-done((f32[320,128]{1,0:T(8,128)S(1)}, f32[320,128]{1,0:T(8,128)S(1)}, u32[]{:S(2)}, u32[]{:S(2)}) %collective-permute-start.3) | collective-permute-done | bytes 163872 | tf_op jit(solution)/shard_map/ppermute | solution.py:539
  67.8 24.1 %whiten.1 = (bf16[64,256,256]{2,1,0:T(8,128)(2,1)}, bf16[64,256,256]{2,1,0:T(8,128)(2,1)}, f32[256,256]{1,0:T(8,128)}) custom-call(f32[640,128]{1,0:T(8,128)S(1)} %pad_maximum_fusion.packed_ref, f32[8,256]{1,0:T(8,128)S(1)} %get-tuple-element.12.pivot_ref, bf16[64,256,256]{2,1,0:T(8,128)(2,1)} %get-tuple-element.15.high_row.high_col.high_from, ...), custom_call_target="tpu_custom_call" | custom-call | flops 6442450944 | bytes 33554432 | tf_op jit(solution)/shard_map/whiten/pallas_call | solution.py:488
  (4 shorter events, 0.1 us)
Async XLA Ops:
  0.6 6.8 %copy-start = (s32[64,256]{1,0:T(8,128)S(1)}, s32[64,256]{1,0:T(8,128)}, u32[]{:S(2)}) copy-start(s32[64,256]{1,0:T(8,128)} %valid_ref.7) | copy-start | bytes 196612
  0.6 6.8 %copy-start.2 = (f32[16,256]{1,0:T(8,128)S(1)}, f32[16,256]{1,0:T(8,128)}, u32[]{:S(2)}) copy-start(f32[16,256]{1,0:T(8,128)} %gains_ref.3) | copy-start | bytes 49156
  0.7 6.8 %copy-start.1 = (s32[64,256]{1,0:T(8,128)S(1)}, s32[64,256]{1,0:T(8,128)}, u32[]{:S(2)}) copy-start(s32[64,256]{1,0:T(8,128)} %class_ref.3) | copy-start | bytes 196612
  2.8 22.5 %collective-permute-start.1 = (f32[64,384]{1,0:T(8,128)}, f32[64,384]{1,0:T(8,128)S(1)}, u32[]{:S(2)}, u32[]{:S(2)}) collective-permute-start(f32[64,384]{1,0:T(8,128)} %get-tuple-element.14), channel_id=1, source_target_pairs={{8,0},{16,8},{24,16},{32,24},{40,32},{48,40},{56,48},{64,56},{72,6... | collective-permute-start | bytes 294920 | tf_op jit(solution)/shard_map/ppermute | solution.py:522
  4.1 21.2 %collective-permute-start = (f32[264,256]{1,0:T(8,128)}, f32[264,256]{1,0:T(8,128)S(1)}, u32[]{:S(2)}, u32[]{:S(2)}) collective-permute-start(f32[264,256]{1,0:T(8,128)} %get-tuple-element.13), channel_id=1, source_target_pairs={{1,0},{2,1},{3,2},{4,3},{5,4},{6,5},{7,6},{9,8},{10,9},{11,10},{12... | collective-permute-start | bytes 811016 | tf_op jit(solution)/shard_map/ppermute | solution.py:522
  27.6 1.5 %collective-permute-start.2 = (f32[320,128]{1,0:T(8,128)S(1)}, f32[320,128]{1,0:T(8,128)S(1)}, u32[]{:S(2)}, u32[]{:S(2)}) collective-permute-start(f32[320,128]{1,0:T(8,128)S(1)} %dynamic-slice_bitcast_fusion), channel_id=1, source_target_pairs={{0,1},{1,0},{2,3},{3,2},{4,5},{5,4},{6,7},{7,6},{8,9},{9,8},{10,11... | collective-permute-start | bytes 491528 | tf_op jit(solution)/shard_map/ppermute | solution.py:535
  64.0 3.7 %collective-permute-start.3 = (f32[320,128]{1,0:T(8,128)S(1)}, f32[320,128]{1,0:T(8,128)S(1)}, u32[]{:S(2)}, u32[]{:S(2)}) collective-permute-start(f32[320,128]{1,0:T(8,128)S(1)} %bitcast.10), channel_id=1, source_target_pairs={{0,1},{1,0},{2,3},{3,2},{4,5},{5,4},{6,7},{7,6},{8,9},{9,8},{10,11... | collective-permute-start | bytes 491528 | tf_op jit(solution)/shard_map/ppermute | solution.py:539

commit v3 on v2

--- a/solution.py
+++ b/solution.py
@@ -91,7 +91,7 @@
 
 
 def moments_kernel(
-    raw_ref, class_ref, valid_ref, gains_ref, high_ref, low_ref, products_ref, sums_ref, pivot_ref, plain, half_degree, terms, gains_bf
+    raw_ref, class_ref, valid_ref, gains_ref, high_ref, low_ref, products_ref, sums_ref, pivot_ref, last_row_ref, last_col_ref, plain, half_degree, terms, gains_bf
 ):
     step = pl.program_id(0)
     count = gains_ref.shape[0]
@@ -137,7 +137,9 @@
             term = above + left - degrees[at : at + CHUNK, row : row + 1] * calibrated
             terms[row * cols + at : row * cols + at + CHUNK, :] = term.astype(BF16)
             total = total + jnp.sum(calibrated.reshape(CHUNK // 8, 8, channels), 0)
+        last_col_ref[pl.ds(start + row, 1), :] = calibrated[CHUNK - 1 :, :]
     sums_ref[...] = total
+    last_row_ref[...] = plain[(STEP_ROWS - 1) % 2, 8:, :]
     pixels = STEP_ROWS * cols
     high = high_ref[...].reshape(pixels, channels)
     products_ref[...] += over_pixels(high, jnp.concatenate([terms[...], high], 1))
@@ -152,13 +154,15 @@
         moments_kernel,
         grid=(rows // STEP_ROWS,),
         in_specs=[block, whole((rows, cols)), whole((rows, cols)), whole(class_gains.shape)],
-        out_specs=[block, block, whole((channels, 2 * channels)), whole((8, channels)), whole((8, channels))],
+        out_specs=[block, block, whole((channels, 2 * channels)), whole((8, channels)), whole((8, channels)), whole((cols, channels)), whole((rows, channels))],
         out_shape=[
             pltpu.HBM(raw_counts.shape, BF16),
             pltpu.HBM(raw_counts.shape, BF16),
             jax.ShapeDtypeStruct((channels, 2 * channels), F32),
             jax.ShapeDtypeStruct((8, channels), F32),
             jax.ShapeDtypeStruct((8, channels), F32),
+            jax.ShapeDtypeStruct((cols, channels), F32),
+            jax.ShapeDtypeStruct((rows, channels), F32),
         ],
         scratch_shapes=[
             pltpu.VMEM((2, 8 + cols, channels), F32),
@@ -175,7 +179,7 @@
 
 
 def pack_kernel(
-    products_ref, sums_ref, pivot_ref, below_ref, right_ref, high_row, low_row, high_col, low_col, valid_ref, packed_ref
+    products_ref, sums_ref, pivot_ref, below_ref, right_ref, last_row_ref, last_col_ref, valid_ref, packed_ref
 ):
     rows, cols = valid_ref.shape
     channels = sums_ref.shape[1]
@@ -183,11 +187,11 @@
     last_valid = as_column(valid[rows - 1 : rows, :])
     below_row = below_ref[cols : cols + 1, :]
     below_valid = as_column(below_row)
-    mine = high_row[0].astype(F32) + low_row[0].astype(F32)
+    mine = last_row_ref[...]
     pivot = pivot_ref[0:1, :]
     down = last_valid * (below_ref[0:cols, :] - below_valid * pivot) - below_valid * mine
     right_valid = right_ref[:, channels : channels + 1]
-    mine = (high_col[...].astype(F32) + low_col[...].astype(F32))[:, 15, :]
+    mine = last_col_ref[...]
     last_col = valid[:, cols - 1 : cols]
     right = last_col * (right_ref[:, :channels] - right_valid * pivot) - right_valid * mine
     edge = jnp.concatenate([down, right], 0).astype(BF16)
@@ -230,11 +234,9 @@
         packed_ref[at + 8 :, :] = jnp.zeros((packed_ref.shape[0] - at - 8, HALF), F32)
 
 
-def pack(products, sums, pivot, below, right, high, low, good_pixels, length):
-    rows, cols, channels = high.shape
+def pack(products, sums, pivot, below, right, last_row, last_col, good_pixels, length):
+    rows, cols = good_pixels.shape
     whole = lambda shape: pl.BlockSpec(shape, lambda i: (0,) * len(shape))
-    last_row = pl.BlockSpec((1, cols, channels), lambda i: (rows - 1, 0, 0))
-    last_col = pl.BlockSpec((rows, 16, channels), lambda i: (0, cols // 16 - 1, 0))
     return pl.pallas_call(
         pack_kernel,
         grid=(1,),
@@ -244,17 +246,15 @@
             whole(pivot.shape),
             whole(below.shape),
             whole(right.shape),
-            last_row,
-            last_row,
-            last_col,
-            last_col,
+            whole(last_row.shape),
+            whole(last_col.shape),
             whole((rows, cols)),
         ],
         out_specs=whole((length, HALF)),
         out_shape=jax.ShapeDtypeStruct((length, HALF), F32),
         compiler_params=pltpu.CompilerParams(vmem_limit_bytes=32 * 1024 * 1024),
         name="pack",
-    )(products, sums, pivot, below, right, high, low, high, low, good_pixels)
+    )(products, sums, pivot, below, right, last_row, last_col, good_pixels)
 
 
 def inverse_of_pair(a, b, c):
@@ -545,11 +545,11 @@
     first_row, first_col = edges(raw_counts, gain_class, good_pixels, class_gains)
     below = from_next(first_row, "row")
     right = from_next(first_col, "col")
-    high, low, products, sums, pivot = moments(raw_counts, gain_class, good_pixels, class_gains)
+    high, low, products, sums, pivot, last_row, last_col = moments(raw_counts, gain_class, good_pixels, class_gains)
     high, low = (pltpu.with_memory_space_constraint(part, pltpu.HBM) for part in (high, low))
     devices = lax.axis_size(("col", "row"))
     length = -(-(4 * HALF + 8) // devices) * devices
-    packed = pack(products, sums, pivot, below, right, high, low, good_pixels, length)
+    packed = pack(products, sums, pivot, below, right, last_row, last_col, good_pixels, length)
     return whiten(summed(packed), pivot, high, low, good_pixels, below, right)
 
 

time: 92.3 us -> 90.9 us (0.985)
  Pallas kernels: 46.3 us -> 45 us
    pallas_call x1, Pallas kernels: 2.27 us -> 0.87 us  [pack(): pl.pallas_call(pack_kernel, grid=(1,), in_specs=[whole(products.shape), w...]
  transfers between devices with their start and end apart: 4 -> 4, of which waited for: 2 -> 2; matrix products, arithmetic and copies ran while one was open for 0% -> 0% of each run, Pallas kernels for 19% -> 20%
where the time goes in v3:
time: 90.9 us; the launch traced here: 90.6 us
  Pallas kernels  45 us (50%)
  blocking collectives  34.7 us (38%)
  starting transfers between devices  7.38 us (8%)
  waiting for transfers between devices  2.41 us (3%)
  between operations  0.91 us (1%)
    pallas_call x1, Pallas kernels, whiten(): pl.pallas_call(whiten_kernel, grid=(steps,), in_specs=[whole(packed.shape...  24.1 us
    all_to_all x1, blocking collectives, summed(): lax.all_to_all(share, axes, 0, 0, axis_index_groups=groups)  21 us
    pallas_call x1, Pallas kernels, moments(): pl.pallas_call(moments_kernel, grid=(rows // STEP_ROWS,), in_specs=[block...  17.9 us
    all_to_all x1, blocking collectives, summed(): lax.all_to_all(jnp.broadcast_to(mine[None], share.shape), axes, 0, 0, axi...  13.7 us
    ppermute x2, starting transfers between devices, from_next(): lax.ppermute(value, axis, [(source, source - 1) for source in range(1, co...  4.61 us
    ppermute x1, starting transfers between devices, summed(): other = lax.ppermute(every, 'row', swap)  2.68 us
    pallas_call x1, Pallas kernels, edges(): pl.pallas_call(edges_kernel, grid=(1,), in_specs=[whole((1, cols, channel...  2.12 us
  transfers between devices with their start and end apart: 4, of which 2 were waited for; matrix products, arithmetic and copies ran while one was open for 0% of the time, Pallas kernels for 20%

profile of v3, /device:TPU:1, one launch (start us, length us, event | category | flops | bytes accessed | tf_op | source)
XLA Modules:
  0.0 90.6 jit_solution(6460008380330168996)
XLA Ops:
  0.6 0.0 copy-start
  0.6 0.0 copy-start.2
  0.7 0.0 copy-start.1
  0.7 2.1 %edges.1 = (f32[264,256]{1,0:T(8,128)}, f32[64,384]{1,0:T(8,128)}) custom-call(bf16[64,256,256]{2,1,0:T(8,128)(2,1)} %col_ref.1, bf16[64,256,256]{2,1,0:T(8,128)(2,1)} %col_ref.1, s32[64,256]{1,0:T(8,128)} %class_ref.3, s32[64,256]{1,0:T(8,128)} %valid_ref.7, f32[16,256]{1,0:T(8,128)} %gains_ref.3), custom_call_target="tpu_custom_call" | custom-call | tf_op jit(solution)/shard_map/edges/pallas_call | solution.py:74
  2.8 1.3 %collective-permute-start.1 = (f32[64,384]{1,0:T(8,128)}, f32[64,384]{1,0:T(8,128)S(1)}, u32[]{:S(2)}, u32[]{:S(2)}) collective-permute-start(f32[64,384]{1,0:T(8,128)} %get-tuple-element.16), channel_id=1, source_target_pairs={{8,0},{16,8},{24,16},{32,24},{40,32},{48,40},{56,48},{64,56},{72,6... | collective-permute-start | bytes 294920 | tf_op jit(solution)/shard_map/ppermute | solution.py:522
  4.1 3.3 %collective-permute-start = (f32[264,256]{1,0:T(8,128)}, f32[264,256]{1,0:T(8,128)S(1)}, u32[]{:S(2)}, u32[]{:S(2)}) collective-permute-start(f32[264,256]{1,0:T(8,128)} %get-tuple-element.15), channel_id=1, source_target_pairs={{1,0},{2,1},{3,2},{4,3},{5,4},{6,5},{7,6},{9,8},{10,9},{11,10},{12... | collective-permute-start | bytes 811016 | tf_op jit(solution)/shard_map/ppermute | solution.py:522
  7.4 0.0 copy-done
  7.4 0.0 copy-done.2
  7.4 0.0 copy-done.1
  7.4 17.9 %moments.1 = (bf16[64,256,256]{2,1,0:T(8,128)(2,1)}, bf16[64,256,256]{2,1,0:T(8,128)(2,1)}, f32[256,512]{1,0:T(8,128)S(1)}, f32[8,256]{1,0:T(8,128)S(1)}, f32[8,...) custom-call(bf16[64,256,256]{2,1,0:T(8,128)(2,1)} %col_ref.1, s32[64,256]{1,0:T(8,128)S(1)} %copy-done.1, ...), custom_call_target="tpu_custom_call" | custom-call | flops 10737418240 | bytes 25165824 | tf_op jit(solution)/shard_map/moments/pallas_call | solution.py:153
  25.3 0.0 collective-permute-done.1.right_ref
  25.3 0.0 collective-permute-done.below_ref
  25.3 0.9 pack.1
  26.2 0.1 collective-permute-start.2
  26.3 1.4 %collective-permute-done.2 = f32[320,128]{1,0:T(8,128)S(1)} collective-permute-done((f32[320,128]{1,0:T(8,128)S(1)}, f32[320,128]{1,0:T(8,128)S(1)}, u32[]{:S(2)}, u32[]{:S(2)}) %collective-permute-start.2) | collective-permute-done | bytes 163872 | tf_op jit(solution)/shard_map/ppermute | solution.py:535
  27.7 21.0 %all_to_all.10 = f32[64,5,1,128]{3,2,1,0:T(1,128)S(1)} all-to-all(f32[64,5,1,128]{3,2,1,0:T(1,128)S(1)} %bitcast.9), channel_id=1, replica_groups={{0,2,4,6,8,10,12,14,16,18,20,22,24,26,28,30,32,34,36,38,40,42,44,46,48,..., dimensions={0} | all-to-all | bytes 327680 | tf_op jit(solution)/shard_map/all_to_all | solution.py:536
  48.7 0.1 reduce_sum.9
  48.8 0.1 broadcast_in_dim.2
  48.9 13.7 %all_to_all.11 = f32[64,5,1,128]{3,2,1,0:T(1,128)S(1)} all-to-all(f32[64,5,1,128]{3,2,1,0:T(1,128)S(1)} %broadcast_in_dim.2), channel_id=1, replica_groups={{0,2,4,6,8,10,12,14,16,18,20,22,24,26,28,30,32,34,36,38,40,42,44,46,48,..., dimensions={0} | all-to-all | bytes 327680 | tf_op jit(solution)/shard_map/all_to_all | solution.py:537
  62.6 2.7 %collective-permute-start.3 = (f32[320,128]{1,0:T(8,128)S(1)}, f32[320,128]{1,0:T(8,128)S(1)}, u32[]{:S(2)}, u32[]{:S(2)}) collective-permute-start(f32[320,128]{1,0:T(8,128)S(1)} %bitcast.10), channel_id=1, source_target_pairs={{0,1},{1,0},{2,3},{3,2},{4,5},{5,4},{6,7},{7,6},{8,9},{9,8},{10,11... | collective-permute-start | bytes 491528 | tf_op jit(solution)/shard_map/ppermute | solution.py:539
  65.3 1.0 %collective-permute-done.3 = f32[320,128]{1,0:T(8,128)S(1)} collective-permute-done((f32[320,128]{1,0:T(8,128)S(1)}, f32[320,128]{1,0:T(8,128)S(1)}, u32[]{:S(2)}, u32[]{:S(2)}) %collective-permute-start.3) | collective-permute-done | bytes 163872 | tf_op jit(solution)/shard_map/ppermute | solution.py:539
  66.4 24.1 %whiten.1 = (bf16[64,256,256]{2,1,0:T(8,128)(2,1)}, bf16[64,256,256]{2,1,0:T(8,128)(2,1)}, f32[256,256]{1,0:T(8,128)}) custom-call(f32[640,128]{1,0:T(8,128)S(1)} %pad_maximum_fusion.packed_ref, f32[8,256]{1,0:T(8,128)S(1)} %get-tuple-element.14.pivot_ref, bf16[64,256,256]{2,1,0:T(8,128)(2,1)} %get-tuple-element.19.high_from, ...), custom_call_target="tpu_custom_call" | custom-call | flops 6442450944 | bytes 33554432 | tf_op jit(solution)/shard_map/whiten/pallas_call | solution.py:488
  (4 shorter events, 0.1 us)
Async XLA Ops:
  0.6 6.8 %copy-start = (s32[64,256]{1,0:T(8,128)S(1)}, s32[64,256]{1,0:T(8,128)}, u32[]{:S(2)}) copy-start(s32[64,256]{1,0:T(8,128)} %valid_ref.7) | copy-start | bytes 196612
  0.6 6.8 %copy-start.2 = (f32[16,256]{1,0:T(8,128)S(1)}, f32[16,256]{1,0:T(8,128)}, u32[]{:S(2)}) copy-start(f32[16,256]{1,0:T(8,128)} %gains_ref.3) | copy-start | bytes 49156
  0.7 6.8 %copy-start.1 = (s32[64,256]{1,0:T(8,128)S(1)}, s32[64,256]{1,0:T(8,128)}, u32[]{:S(2)}) copy-start(s32[64,256]{1,0:T(8,128)} %class_ref.3) | copy-start | bytes 196612
  2.8 22.5 %collective-permute-start.1 = (f32[64,384]{1,0:T(8,128)}, f32[64,384]{1,0:T(8,128)S(1)}, u32[]{:S(2)}, u32[]{:S(2)}) collective-permute-start(f32[64,384]{1,0:T(8,128)} %get-tuple-element.16), channel_id=1, source_target_pairs={{8,0},{16,8},{24,16},{32,24},{40,32},{48,40},{56,48},{64,56},{72,6... | collective-permute-start | bytes 294920 | tf_op jit(solution)/shard_map/ppermute | solution.py:522
  4.1 21.2 %collective-permute-start = (f32[264,256]{1,0:T(8,128)}, f32[264,256]{1,0:T(8,128)S(1)}, u32[]{:S(2)}, u32[]{:S(2)}) collective-permute-start(f32[264,256]{1,0:T(8,128)} %get-tuple-element.15), channel_id=1, source_target_pairs={{1,0},{2,1},{3,2},{4,3},{5,4},{6,5},{7,6},{9,8},{10,9},{11,10},{12... | collective-permute-start | bytes 811016 | tf_op jit(solution)/shard_map/ppermute | solution.py:522
  26.2 1.5 %collective-permute-start.2 = (f32[320,128]{1,0:T(8,128)S(1)}, f32[320,128]{1,0:T(8,128)S(1)}, u32[]{:S(2)}, u32[]{:S(2)}) collective-permute-start(f32[320,128]{1,0:T(8,128)S(1)} %dynamic-slice_bitcast_fusion), channel_id=1, source_target_pairs={{0,1},{1,0},{2,3},{3,2},{4,5},{5,4},{6,7},{7,6},{8,9},{9,8},{10,11... | collective-permute-start | bytes 491528 | tf_op jit(solution)/shard_map/ppermute | solution.py:535
  62.6 3.7 %collective-permute-start.3 = (f32[320,128]{1,0:T(8,128)S(1)}, f32[320,128]{1,0:T(8,128)S(1)}, u32[]{:S(2)}, u32[]{:S(2)}) collective-permute-start(f32[320,128]{1,0:T(8,128)S(1)} %bitcast.10), channel_id=1, source_target_pairs={{0,1},{1,0},{2,3},{3,2},{4,5},{5,4},{6,7},{7,6},{8,9},{9,8},{10,11... | collective-permute-start | bytes 491528 | tf_op jit(solution)/shard_map/ppermute | solution.py:539

commit v4 on v3

--- a/solution.py
+++ b/solution.py
@@ -7,6 +7,8 @@
 
 STEP_ROWS = 16
 CHUNK = 32
+GROUP = 4
+GROUPS = STEP_ROWS // GROUP
 HALF = 128
 HIGHEST = lax.Precision.HIGHEST
 F32 = jnp.float32
@@ -38,6 +40,18 @@
     middle = rest.astype(BF16)
     low = (rest - middle.astype(F32)).astype(BF16)
     return jnp.concatenate([high, middle, low], 0)
+
+
+def sends(pairs, sent, slot, start, groups=range(GROUPS)):
+    return [
+        pltpu.make_async_copy(
+            buffer.at[slot, pl.ds(GROUP * group, GROUP)],
+            target.at[pl.ds(start + GROUP * group, GROUP)],
+            sent.at[which, slot, group],
+        )
+        for group in groups
+        for which, (buffer, target) in enumerate(pairs)
+    ]
 
 
 def row_gains(classes, valid, gains, count):
@@ -91,7 +105,7 @@
 
 
 def moments_kernel(
-    raw_ref, class_ref, valid_ref, gains_ref, high_ref, low_ref, products_ref, sums_ref, pivot_ref, last_row_ref, last_col_ref, plain, half_degree, terms, gains_bf
+    raw_ref, class_ref, valid_ref, gains_ref, high_to, low_to, products_ref, sums_ref, pivot_ref, last_row_ref, last_col_ref, plain, half_degree, terms, gains_bf, high_ref, low_ref, sent
 ):
     step = pl.program_id(0)
     count = gains_ref.shape[0]
@@ -118,6 +132,14 @@
     start = pl.multiple_of(step * STEP_ROWS, STEP_ROWS)
     classes = class_ref[pl.ds(start, STEP_ROWS), :]
     valid = valid_ref[pl.ds(start, STEP_ROWS), :]
+    slot = lax.rem(step, 2)
+    pairs = ((high_ref, high_to), (low_ref, low_to))
+
+    @pl.when(step >= 2)
+    def _():
+        for copy in sends(pairs, sent, slot, start - 2 * STEP_ROWS):
+            copy.wait()
+
     degrees = jnp.transpose(half_degree[pl.ds(start, STEP_ROWS), :])
     valid_cols = jnp.transpose(valid.astype(F32))
     pivot = pivot_ref[0:1, :]
@@ -129,8 +151,8 @@
             calibrated = raw_ref[row, at : at + CHUNK, :].astype(F32) * gain_map[at : at + CHUNK]
             calibrated = calibrated - valid_cols[at : at + CHUNK, row : row + 1] * pivot
             high, low = split(calibrated)
-            high_ref[row, at : at + CHUNK, :] = high
-            low_ref[row, at : at + CHUNK, :] = low
+            high_ref[slot, row, at : at + CHUNK, :] = high
+            low_ref[slot, row, at : at + CHUNK, :] = low
             plain[row % 2, 8 + at : 8 + at + CHUNK, :] = calibrated
             left = plain[row % 2, 7 + at : 7 + at + CHUNK, :]
             above = plain[1 - row % 2, 8 + at : 8 + at + CHUNK, :]
@@ -138,11 +160,23 @@
             terms[row * cols + at : row * cols + at + CHUNK, :] = term.astype(BF16)
             total = total + jnp.sum(calibrated.reshape(CHUNK // 8, 8, channels), 0)
         last_col_ref[pl.ds(start + row, 1), :] = calibrated[CHUNK - 1 :, :]
+        if row % GROUP == GROUP - 1:
+            for copy in sends(pairs, sent, slot, start, [row // GROUP]):
+                copy.start()
     sums_ref[...] = total
     last_row_ref[...] = plain[(STEP_ROWS - 1) % 2, 8:, :]
     pixels = STEP_ROWS * cols
-    high = high_ref[...].reshape(pixels, channels)
+    high = high_ref[slot].reshape(pixels, channels)
     products_ref[...] += over_pixels(high, jnp.concatenate([terms[...], high], 1))
+    steps = rows // STEP_ROWS
+
+    @pl.when(step == steps - 1)
+    def _():
+        if steps > 1:
+            for copy in sends(pairs, sent, 1 - slot, start - STEP_ROWS):
+                copy.wait()
+        for copy in sends(pairs, sent, slot, start):
+            copy.wait()
 
 
 def moments(raw_counts, gain_class, good_pixels, class_gains):
@@ -154,7 +188,7 @@
         moments_kernel,
         grid=(rows // STEP_ROWS,),
         in_specs=[block, whole((rows, cols)), whole((rows, cols)), whole(class_gains.shape)],
-        out_specs=[block, block, whole((channels, 2 * channels)), whole((8, channels)), whole((8, channels)), whole((cols, channels)), whole((rows, channels))],
+        out_specs=[pl.BlockSpec(memory_space=pl.ANY)] * 2 + [whole((channels, 2 * channels)), whole((8, channels)), whole((8, channels)), whole((cols, channels)), whole((rows, channels))],
         out_shape=[
             pltpu.HBM(raw_counts.shape, BF16),
             pltpu.HBM(raw_counts.shape, BF16),
@@ -169,6 +203,9 @@
             pltpu.VMEM((rows, cols), F32),
             pltpu.VMEM((STEP_ROWS * cols, channels), BF16),
             pltpu.VMEM((3 * class_gains.shape[0], channels), BF16),
+            pltpu.VMEM((2, STEP_ROWS, cols, channels), BF16),
+            pltpu.VMEM((2, STEP_ROWS, cols, channels), BF16),
+            pltpu.SemaphoreType.DMA((2, 2, GROUPS)),
         ],
         compiler_params=pltpu.CompilerParams(vmem_limit_bytes=32 * 1024 * 1024),
         cost_estimate=pl.CostEstimate(
@@ -420,8 +457,8 @@
     valid_ref,
     below_ref,
     right_ref,
-    white_ref,
-    noise_ref,
+    white_to,
+    noise_to,
     factor_ref,
     high_ref,
     low_ref,
@@ -431,10 +468,13 @@
     right_edge,
     neighbours,
     arrived,
+    white_ref,
+    noise_ref,
+    sent,
 ):
     step = pl.program_id(0)
-    steps = pl.num_programs(0)
     rows, cols = valid_ref.shape
+    steps = rows // STEP_ROWS
     channels = high_ref.shape[2]
 
     @pl.when(step == 0)
@@ -459,6 +499,14 @@
             copy.wait()
 
     start = pl.multiple_of((steps - 1 - step) * STEP_ROWS, STEP_ROWS)
+    slot = lax.rem(step, 2)
+    pairs = ((white_ref, white_to), (noise_ref, noise_to))
+
+    @pl.when(step >= 2)
+    def _():
+        for copy in sends(pairs, sent, slot, start + 2 * STEP_ROWS):
+            copy.wait()
+
     valid = jnp.transpose(valid_ref[pl.ds(start, STEP_ROWS), :].astype(F32))
     number = jnp.transpose(neighbours[pl.ds(start, STEP_ROWS), :])
     edge = right_edge[pl.ds(start, STEP_ROWS), :]
@@ -473,10 +521,21 @@
             right = plain[base + at + 1 : base + at + 1 + CHUNK, :]
             below = plain[base + cols + 8 + at : base + cols + 8 + at + CHUNK, :]
             ok = valid[at : at + CHUNK, row : row + 1]
-            white_ref[row, at : at + CHUNK, :] = (here - ok * offset).astype(BF16)
+            white_ref[slot, row, at : at + CHUNK, :] = (here - ok * offset).astype(BF16)
             around = number[at : at + CHUNK, row : row + 1]
-            noise_ref[row, at : at + CHUNK, :] = (ok * (below + right) - around * here).astype(BF16)
+            noise_ref[slot, row, at : at + CHUNK, :] = (ok * (below + right) - around * here).astype(BF16)
+        if row % GROUP == 0:
+            for copy in sends(pairs, sent, slot, start, [row // GROUP]):
+                copy.start()
     plain[STEP_ROWS * (cols + 8) :, :] = plain[0 : cols, :]
+
+    @pl.when(step == steps - 1)
+    def _():
+        if steps > 1:
+            for copy in sends(pairs, sent, 1 - slot, start + STEP_ROWS):
+                copy.wait()
+        for copy in sends(pairs, sent, slot, start):
+            copy.wait()
 
 
 def whiten(packed, pivot, high, low, good_pixels, below, right):
@@ -484,7 +543,6 @@
     steps = rows // STEP_ROWS
     pixels = rows * cols
     whole = lambda shape: pl.BlockSpec(shape, lambda i: (0,) * len(shape))
-    block = pl.BlockSpec((STEP_ROWS, cols, channels), lambda i: (steps - 1 - i, 0, 0))
     return pl.pallas_call(
         whiten_kernel,
         grid=(steps,),
@@ -497,7 +555,7 @@
             whole(below.shape),
             whole(right.shape),
         ],
-        out_specs=[block, block, whole((channels, channels))],
+        out_specs=[pl.BlockSpec(memory_space=pl.ANY)] * 2 + [whole((channels, channels))],
         out_shape=[jax.ShapeDtypeStruct(high.shape, BF16)] * 2 + [jax.ShapeDtypeStruct((channels, channels), F32)],
         scratch_shapes=[
             pltpu.VMEM(high.shape, BF16),
@@ -508,6 +566,9 @@
             pltpu.VMEM((rows, channels), F32),
             pltpu.VMEM((rows, cols), F32),
             pltpu.SemaphoreType.DMA((2,)),
+            pltpu.VMEM((2, STEP_ROWS, cols, channels), BF16),
+            pltpu.VMEM((2, STEP_ROWS, cols, channels), BF16),
+            pltpu.SemaphoreType.DMA((2, 2, GROUPS)),
         ],
         compiler_params=pltpu.CompilerParams(vmem_limit_bytes=48 * 1024 * 1024),
         cost_estimate=pl.CostEstimate(

time: 90.9 us -> 91.2 us (level)
  no operation moved by 1% of the time
where the time goes in v4:
time: 91.2 us; the launch traced here: 90.9 us
  Pallas kernels  45.2 us (50%)
  blocking collectives  34.7 us (38%)
  starting transfers between devices  7.38 us (8%)
  waiting for transfers between devices  2.41 us (3%)
  between operations  0.94 us (1%)
    pallas_call x1, Pallas kernels, whiten(): pl.pallas_call(whiten_kernel, grid=(steps,), in_specs=[whole(packed.shape...  24 us
    all_to_all x1, blocking collectives, summed(): lax.all_to_all(share, axes, 0, 0, axis_index_groups=groups)  21 us
    pallas_call x1, Pallas kernels, moments(): pl.pallas_call(moments_kernel, grid=(rows // STEP_ROWS,), in_specs=[block...  18.2 us
    all_to_all x1, blocking collectives, summed(): lax.all_to_all(jnp.broadcast_to(mine[None], share.shape), axes, 0, 0, axi...  13.7 us
    ppermute x2, starting transfers between devices, from_next(): lax.ppermute(value, axis, [(source, source - 1) for source in range(1, co...  4.61 us
    ppermute x1, starting transfers between devices, summed(): other = lax.ppermute(every, 'row', swap)  2.68 us
    pallas_call x1, Pallas kernels, edges(): pl.pallas_call(edges_kernel, grid=(1,), in_specs=[whole((1, cols, channel...  2.12 us
  transfers between devices with their start and end apart: 4, of which 2 were waited for; matrix products, arithmetic and copies ran while one was open for 0% of the time, Pallas kernels for 20%

profile of v4, /device:TPU:1, one launch (start us, length us, event | category | flops | bytes accessed | tf_op | source)
XLA Modules:
  0.0 90.9 jit_solution(11153644636408497592)
XLA Ops:
  0.6 0.0 copy-start
  0.6 0.0 copy-start.2
  0.7 0.0 copy-start.1
  0.7 2.1 %edges.1 = (f32[264,256]{1,0:T(8,128)}, f32[64,384]{1,0:T(8,128)}) custom-call(bf16[64,256,256]{2,1,0:T(8,128)(2,1)} %col_ref.1, bf16[64,256,256]{2,1,0:T(8,128)(2,1)} %col_ref.1, s32[64,256]{1,0:T(8,128)} %class_ref.3, s32[64,256]{1,0:T(8,128)} %valid_ref.7, f32[16,256]{1,0:T(8,128)} %gains_ref.3), custom_call_target="tpu_custom_call" | custom-call | tf_op jit(solution)/shard_map/edges/pallas_call | solution.py:88
  2.8 1.3 %collective-permute-start.1 = (f32[64,384]{1,0:T(8,128)}, f32[64,384]{1,0:T(8,128)S(1)}, u32[]{:S(2)}, u32[]{:S(2)}) collective-permute-start(f32[64,384]{1,0:T(8,128)} %get-tuple-element.16), channel_id=1, source_target_pairs={{8,0},{16,8},{24,16},{32,24},{40,32},{48,40},{56,48},{64,56},{72,6... | collective-permute-start | bytes 294920 | tf_op jit(solution)/shard_map/ppermute | solution.py:583
  4.1 3.3 %collective-permute-start = (f32[264,256]{1,0:T(8,128)}, f32[264,256]{1,0:T(8,128)S(1)}, u32[]{:S(2)}, u32[]{:S(2)}) collective-permute-start(f32[264,256]{1,0:T(8,128)} %get-tuple-element.15), channel_id=1, source_target_pairs={{1,0},{2,1},{3,2},{4,3},{5,4},{6,5},{7,6},{9,8},{10,9},{11,10},{12... | collective-permute-start | bytes 811016 | tf_op jit(solution)/shard_map/ppermute | solution.py:583
  7.4 0.0 copy-done
  7.4 0.0 copy-done.2
  7.4 0.0 copy-done.1
  7.4 18.2 %moments.1 = (bf16[64,256,256]{2,1,0:T(8,128)(2,1)}, bf16[64,256,256]{2,1,0:T(8,128)(2,1)}, f32[256,512]{1,0:T(8,128)S(1)}, f32[8,256]{1,0:T(8,128)S(1)}, f32[8,...) custom-call(bf16[64,256,256]{2,1,0:T(8,128)(2,1)} %col_ref.1, s32[64,256]{1,0:T(8,128)S(1)} %copy-done.1, ...), custom_call_target="tpu_custom_call" | custom-call | flops 10737418240 | bytes 25165824 | tf_op jit(solution)/shard_map/moments/pallas_call | solution.py:187
  25.7 0.0 collective-permute-done.1.right_ref
  25.7 0.0 collective-permute-done.below_ref
  25.7 0.9 pack.1
  26.6 0.1 collective-permute-start.2
  26.7 1.4 %collective-permute-done.2 = f32[320,128]{1,0:T(8,128)S(1)} collective-permute-done((f32[320,128]{1,0:T(8,128)S(1)}, f32[320,128]{1,0:T(8,128)S(1)}, u32[]{:S(2)}, u32[]{:S(2)}) %collective-permute-start.2) | collective-permute-done | bytes 163872 | tf_op jit(solution)/shard_map/ppermute | solution.py:596
  28.1 21.0 %all_to_all.10 = f32[64,5,1,128]{3,2,1,0:T(1,128)S(1)} all-to-all(f32[64,5,1,128]{3,2,1,0:T(1,128)S(1)} %bitcast.9), channel_id=1, replica_groups={{0,2,4,6,8,10,12,14,16,18,20,22,24,26,28,30,32,34,36,38,40,42,44,46,48,..., dimensions={0} | all-to-all | bytes 327680 | tf_op jit(solution)/shard_map/all_to_all | solution.py:597
  49.1 0.1 reduce_sum.9
  49.2 0.1 broadcast_in_dim.2
  49.3 13.7 %all_to_all.11 = f32[64,5,1,128]{3,2,1,0:T(1,128)S(1)} all-to-all(f32[64,5,1,128]{3,2,1,0:T(1,128)S(1)} %broadcast_in_dim.2), channel_id=1, replica_groups={{0,2,4,6,8,10,12,14,16,18,20,22,24,26,28,30,32,34,36,38,40,42,44,46,48,..., dimensions={0} | all-to-all | bytes 327680 | tf_op jit(solution)/shard_map/all_to_all | solution.py:598
  63.0 2.7 %collective-permute-start.3 = (f32[320,128]{1,0:T(8,128)S(1)}, f32[320,128]{1,0:T(8,128)S(1)}, u32[]{:S(2)}, u32[]{:S(2)}) collective-permute-start(f32[320,128]{1,0:T(8,128)S(1)} %bitcast.10), channel_id=1, source_target_pairs={{0,1},{1,0},{2,3},{3,2},{4,5},{5,4},{6,7},{7,6},{8,9},{9,8},{10,11... | collective-permute-start | bytes 491528 | tf_op jit(solution)/shard_map/ppermute | solution.py:600
  65.7 1.0 %collective-permute-done.3 = f32[320,128]{1,0:T(8,128)S(1)} collective-permute-done((f32[320,128]{1,0:T(8,128)S(1)}, f32[320,128]{1,0:T(8,128)S(1)}, u32[]{:S(2)}, u32[]{:S(2)}) %collective-permute-start.3) | collective-permute-done | bytes 163872 | tf_op jit(solution)/shard_map/ppermute | solution.py:600
  66.8 24.0 %whiten.1 = (bf16[64,256,256]{2,1,0:T(8,128)(2,1)}, bf16[64,256,256]{2,1,0:T(8,128)(2,1)}, f32[256,256]{1,0:T(8,128)}) custom-call(f32[640,128]{1,0:T(8,128)S(1)} %pad_maximum_fusion.packed_ref, f32[8,256]{1,0:T(8,128)S(1)} %get-tuple-element.14.pivot_ref, bf16[64,256,256]{2,1,0:T(8,128)(2,1)} %get-tuple-element.19.high_from, ...), custom_call_target="tpu_custom_call" | custom-call | flops 6442450944 | bytes 33554432 | tf_op jit(solution)/shard_map/whiten/pallas_call | solution.py:546
  (4 shorter events, 0.1 us)
Async XLA Ops:
  0.6 6.8 %copy-start = (s32[64,256]{1,0:T(8,128)S(1)}, s32[64,256]{1,0:T(8,128)}, u32[]{:S(2)}) copy-start(s32[64,256]{1,0:T(8,128)} %valid_ref.7) | copy-start | bytes 196612
  0.6 6.8 %copy-start.2 = (f32[16,256]{1,0:T(8,128)S(1)}, f32[16,256]{1,0:T(8,128)}, u32[]{:S(2)}) copy-start(f32[16,256]{1,0:T(8,128)} %gains_ref.3) | copy-start | bytes 49156
  0.7 6.8 %copy-start.1 = (s32[64,256]{1,0:T(8,128)S(1)}, s32[64,256]{1,0:T(8,128)}, u32[]{:S(2)}) copy-start(s32[64,256]{1,0:T(8,128)} %class_ref.3) | copy-start | bytes 196612
  2.8 22.9 %collective-permute-start.1 = (f32[64,384]{1,0:T(8,128)}, f32[64,384]{1,0:T(8,128)S(1)}, u32[]{:S(2)}, u32[]{:S(2)}) collective-permute-start(f32[64,384]{1,0:T(8,128)} %get-tuple-element.16), channel_id=1, source_target_pairs={{8,0},{16,8},{24,16},{32,24},{40,32},{48,40},{56,48},{64,56},{72,6... | collective-permute-start | bytes 294920 | tf_op jit(solution)/shard_map/ppermute | solution.py:583
  4.1 21.6 %collective-permute-start = (f32[264,256]{1,0:T(8,128)}, f32[264,256]{1,0:T(8,128)S(1)}, u32[]{:S(2)}, u32[]{:S(2)}) collective-permute-start(f32[264,256]{1,0:T(8,128)} %get-tuple-element.15), channel_id=1, source_target_pairs={{1,0},{2,1},{3,2},{4,3},{5,4},{6,5},{7,6},{9,8},{10,9},{11,10},{12... | collective-permute-start | bytes 811016 | tf_op jit(solution)/shard_map/ppermute | solution.py:583
  26.6 1.5 %collective-permute-start.2 = (f32[320,128]{1,0:T(8,128)S(1)}, f32[320,128]{1,0:T(8,128)S(1)}, u32[]{:S(2)}, u32[]{:S(2)}) collective-permute-start(f32[320,128]{1,0:T(8,128)S(1)} %dynamic-slice_bitcast_fusion), channel_id=1, source_target_pairs={{0,1},{1,0},{2,3},{3,2},{4,5},{5,4},{6,7},{7,6},{8,9},{9,8},{10,11... | collective-permute-start | bytes 491528 | tf_op jit(solution)/shard_map/ppermute | solution.py:596
  63.0 3.7 %collective-permute-start.3 = (f32[320,128]{1,0:T(8,128)S(1)}, f32[320,128]{1,0:T(8,128)S(1)}, u32[]{:S(2)}, u32[]{:S(2)}) collective-permute-start(f32[320,128]{1,0:T(8,128)S(1)} %bitcast.10), channel_id=1, source_target_pairs={{0,1},{1,0},{2,3},{3,2},{4,5},{5,4},{6,7},{7,6},{8,9},{9,8},{10,11... | collective-permute-start | bytes 491528 | tf_op jit(solution)/shard_map/ppermute | solution.py:600
